TPU v7x, 128 devices: a whole 4x4x4 slice. The times are simulated.
128 devices in a mesh: row: 16 (over x, y), col: 8 (over z, core).
Axes of the slice: x: 4, y: 4, z: 4, core: 2. Of those that a mesh axis runs over, the one named last changes fastest.
Arguments:
- tokens: bfloat16 [1024, 12288], P('col', 'row'), may hold values from -6 to 6
- grad_out: bfloat16 [1024, 12288], P('col', 'row'), may hold values from -6 to 6
- up_weight: bfloat16 [12288, 24576], P('row', 'col'), may hold values from -0.0546875 to 0.0546875
- down_weight: bfloat16 [24576, 12288], P('col', 'row'), may hold values from -0.0390625 to 0.0390625
- up_bias: float32 [24576], P('col'), may hold values from -4 to 4
- relu_bits: int32 [1024, 1536], P('row', 'col'), may hold values from 0 to 65535
- drop_bits: int32 [1024, 1536], P('row', 'col'), may hold values from 0 to 65535, as said below
Outputs:
- grad_tokens: bfloat16 [1024, 12288], P('col', 'row')
- grad_up: bfloat16 [12288, 24576], P('row', 'col')
- grad_down: bfloat16 [24576, 12288], P('col', 'row')
- grad_bias: float32 [24576], P('col')
Inputs may be any that keep to these rules, and one draw needn't show every extreme that they name: `relu_bits`: bit k of word j of token t is the saved ReLU mask of hidden unit 16 j + k. `drop_bits`: bit k of word j of token t is 1 where dropout kept hidden unit 16 j + k of token t.
All inputs are finite; a program needn't handle non-finite values.
Results may differ from a plain program's by a relative error of at most 0.03.
Values may be sent and summed in bfloat16 or wider, within the bound.
A program may use at most 128 MiB of HBM per device.

v0:
```python
import math

import jax
import jax.numpy as jnp
from jax import lax
from jax.sharding import PartitionSpec as P

keep_rate = 0.9


def unpack(words):
    shifts = jnp.arange(16, dtype=jnp.int32)
    bits = jnp.right_shift(words[:, :, None], shifts[None, None, :]) & 1
    return bits.reshape(words.shape[0], words.shape[1] * 16).astype(jnp.float32)


def contract_rows(left, right):
    return lax.dot_general(
        left, right, (((0,), (0,)), ((), ())), preferred_element_type=jnp.float32
    )


def contract_cols(left, right):
    return lax.dot_general(
        left, right, (((1,), (1,)), ((), ())), preferred_element_type=jnp.float32
    )


def body(tokens, grad_out, up_weight, down_weight, up_bias, relu_bits, drop_bits):
    acts, grads = (
        lax.all_gather(tokens, "col", axis=0, tiled=True),
        lax.all_gather(grad_out, "col", axis=0, tiled=True),
    )
    total = acts.shape[0]
    width = up_weight.shape[1]
    scale = 1.0 / math.sqrt(total)
    pre_part = jnp.dot(acts, up_weight, preferred_element_type=jnp.float32)
    back_part = contract_cols(grads, down_weight)
    summed = lax.psum_scatter(
        jnp.concatenate([pre_part, back_part], axis=1).astype(jnp.bfloat16),
        "row",
        scatter_dimension=0,
        tiled=True,
    ).astype(jnp.float32)
    keep = unpack(relu_bits) * unpack(drop_bits) * (1.0 / keep_rate)
    hidden = (keep * (summed[:, :width] + up_bias[None, :])).astype(jnp.bfloat16)
    grad_pre = (keep * summed[:, width:]).astype(jnp.bfloat16)
    bias_local = jnp.sum(grad_pre.astype(jnp.float32), axis=0)
    bias_total = lax.psum(bias_local, "row")
    hidden_all, grad_pre_all = (
        lax.all_gather(hidden, "row", axis=0, tiled=True),
        lax.all_gather(grad_pre, "row", axis=0, tiled=True),
    )
    grad_up = (contract_rows(acts, grad_pre_all) * scale).astype(jnp.bfloat16)
    grad_down = (contract_rows(hidden_all, grads) * scale).astype(jnp.bfloat16)
    grad_tokens = lax.psum_scatter(
        contract_cols(grad_pre_all, up_weight).astype(jnp.bfloat16),
        "col",
        scatter_dimension=0,
        tiled=True,
    )
    grad_bias = bias_total * scale
    return (grad_tokens, grad_up, grad_down, grad_bias)


def solution(mesh):
    return jax.shard_map(
        body,
        mesh=mesh,
        in_specs=(
            P("col", "row"),
            P("col", "row"),
            P("row", "col"),
            P("col", "row"),
            P("col"),
            P("row", "col"),
            P("row", "col"),
        ),
        out_specs=(P("col", "row"), P("row", "col"), P("col", "row"), P("col")),
        check_vma=False,
    )
```

profile of v0, /device:TPU:0, one launch (start us, length us, event | category | flops | bytes accessed | tf_op | source)
XLA Modules:
  0.0 342.9 jit_solution(17004976521510193702)
XLA Ops:
  7.2 0.0 all-gather.7.cloned.1.call-start
  7.2 0.7 all-gather.7.cloned.1.call-update
  7.9 0.0 all-gather.5.cloned.1.call-start
  7.9 0.7 all-gather.5.cloned.1.call-update
  8.6 0.0 reduce-scatter.3.cloned.1.call-start
  8.7 28.0 %all-gather.7.cloned.1.call-done = bf16[1024,768]{1,0:T(8,128)(2,1)} async-done(((bf16[128,768]{1,0:T(8,128)(2,1)}), bf16[1024,768]{1,0:T(8,128)(2,1)}) %all-gather.7.cloned.1.call-update) | async-done | bytes 1572880 | tf_op jit(solution)/shard_map/all_gather | solution.py:32
  36.7 9.2 %convolution_convert_fusion = bf16[1024,3072]{1,0:T(8,128)(2,1)} fusion(bf16[1024,768]{1,0:T(8,128)(2,1)} %all-gather.7.cloned.1.call-done, bf16[3072,768]{1,0:T(8,128)(2,1)} %param.10), kind=kOutput, calls=%fused_computation.3 | convolution fusion | flops 4834983936 | bytes 12582912 | tf_op jit(solution)/shard_map/dot_general | solution.py:24
  45.9 17.1 %all-gather.5.cloned.1.call-done = bf16[1024,768]{1,0:T(8,128)(2,1)} async-done(((bf16[128,768]{1,0:T(8,128)(2,1)}), bf16[1024,768]{1,0:T(8,128)(2,1)}) %all-gather.5.cloned.1.call-update) | async-done | bytes 1572880 | tf_op jit(solution)/shard_map/all_gather | solution.py:31
  63.0 0.0 copy-start
  63.0 7.5 %convolution_convert_fusion.1 = bf16[1024,3072]{1,0:T(8,128)(2,1)S(1)} fusion(bf16[1024,768]{1,0:T(8,128)(2,1)} %all-gather.5.cloned.1.call-done, bf16[768,3072]{1,0:T(8,128)(2,1)} %param.9), kind=kOutput, calls=%fused_computation.4 | convolution fusion | flops 4834983936 | bytes 12582912 | tf_op jit(solution)/shard_map/dot_general | solution.py:37
  70.5 0.0 copy-done
  70.6 8.8 %pad_maximum_fusion = bf16[1024,6144]{1,0:T(8,128)(2,1)} fusion(bf16[1024,3072]{1,0:T(8,128)(2,1)S(1)} %copy-done, bf16[1024,3072]{1,0:T(8,128)(2,1)S(1)} %convolution_convert_fusion.1), kind=kLoop, calls=%fused_computation | loop fusion | flops 25165824 | bytes 25165824 | tf_op jit(solution)/shard_map/concatenate | solution.py:40
  79.4 0.0 copy-start.1
  79.4 0.0 copy-start.2
  79.4 0.0 reduce-scatter.3.cloned.1.call-update
  79.4 0.0 all-gather.9.cloned.1.call-start
  79.5 0.8 copy-done.1
  80.2 0.1 copy.12
  80.3 0.1 shift_right_arithmetic.40
  80.4 0.0 copy-start.3
  80.4 0.4 copy.13
  80.9 0.0 copy-done.2
  80.9 0.1 copy.14
  81.0 0.1 shift_right_arithmetic.46
  81.1 0.4 copy.15
  81.6 0.1 shift_right_arithmetic.43
  81.7 92.4 %reduce-scatter.3.cloned.1.call-done = bf16[64,6144]{1,0:T(8,128)(2,1)} async-done(((bf16[1024,6144]{1,0:T(8,128)(2,1)}), bf16[64,6144]{1,0:T(8,128)(2,1)}) %reduce-scatter.3.cloned.1.call-update) | async-done | bytes 786448 | tf_op jit(solution)/shard_map/reduce_scatter | solution.py:39
  174.1 1.2 convert_element_type.33
  175.3 0.0 copy-done.3
  175.4 1.2 convert_reduce_fusion
  176.6 0.0 all-gather.9.cloned.1.call-update
  176.6 0.0 all-gather.11.cloned.1.call-start
  176.6 0.5 all-gather.11.cloned.1.call-update
  177.2 0.0 reduce-scatter.5.cloned.1.call-start
  177.2 72.6 %psum.7 = f32[3072]{0:T(1024)S(1)} all-reduce(f32[3072]{0:T(1024)S(1)} %get-tuple-element.12), channel_id=1, replica_groups=mesh['row'=16,'col'=8] {'row'}, use_global_device_ids=true, to_apply=%region_3.0 | all-reduce | flops 3072 | bytes 24576 | tf_op jit(solution)/shard_map/psum | solution.py:49
  249.9 0.6 broadcast_multiply_fusion
  250.5 0.0 copy-start.5
  250.5 0.0 all-gather.9.cloned.1.call-done
  250.5 9.6 %convolution_convert_fusion.2 = bf16[1024,768]{1,0:T(8,128)(2,1)} fusion(bf16[1024,3072]{1,0:T(8,128)(2,1)} %all-gather.9.cloned.1.call-done, bf16[768,3072]{1,0:T(8,128)(2,1)} %param.9), kind=kOutput, calls=%fused_computation.6 | convolution fusion | flops 4832624640 | bytes 12582912 | tf_op jit(solution)/shard_map/dot_general | solution.py:24
  260.0 0.0 reduce-scatter.5.cloned.1.call-update
  260.1 0.0 copy-done.5
  260.1 9.8 %fusion = bf16[768,3072]{0,1:T(8,128)(2,1)} fusion(bf16[1024,3072]{1,0:T(8,128)(2,1)} %all-gather.9.cloned.1.call-done, bf16[1024,768]{1,0:T(8,128)(2,1)S(1)} %copy-done.5), kind=kOutput, calls=%fused_computation.5 | convolution fusion | flops 4836556800 | bytes 12582912 | tf_op jit(solution)/shard_map/dot_general | solution.py:18
  269.9 0.0 copy-start.4
  269.9 6.8 %copy.16 = bf16[768,3072]{1,0:T(8,128)(2,1)} copy(bf16[768,3072]{0,1:T(8,128)(2,1)} %fusion) | data formatting | bytes 9437184
  276.6 23.9 %all-gather.11.cloned.1.call-done = bf16[1024,3072]{1,0:T(8,128)(2,1)} async-done(((bf16[64,3072]{1,0:T(8,128)(2,1)}), bf16[1024,3072]{1,0:T(8,128)(2,1)}) %all-gather.11.cloned.1.call-update) | async-done | bytes 6291472 | tf_op jit(solution)/shard_map/all_gather | solution.py:51
  300.6 0.0 copy-done.4
  300.6 9.7 %multiply_convert_fusion = bf16[3072,768]{1,0:T(8,128)(2,1)} fusion(bf16[1024,3072]{1,0:T(8,128)(2,1)} %all-gather.11.cloned.1.call-done, bf16[1024,768]{1,0:T(8,128)(2,1)S(1)} %copy-done.4), kind=kOutput, calls=%fused_computation.1 | convolution fusion | flops 4836556800 | bytes 12582912 | tf_op jit(solution)/shard_map/dot_general | solution.py:18
  310.2 25.8 %reduce-scatter.5.cloned.1.call-done = bf16[128,768]{1,0:T(8,128)(2,1)} async-done(((bf16[1024,768]{1,0:T(8,128)(2,1)}), bf16[128,768]{1,0:T(8,128)(2,1)}) %reduce-scatter.5.cloned.1.call-update) | async-done | bytes 196624 | tf_op jit(solution)/shard_map/reduce_scatter | solution.py:56
  (1 shorter events, 0.0 us)
Async XLA Ops:
  7.2 29.6 %all-gather.7.cloned.1.call-start = ((), (), s32[]{:S(2)}) async-start(), calls=%async_computation.3 | async-start | bytes 1769472 | tf_op jit(solution)/shard_map/all_gather | solution.py:32
  7.9 55.1 %all-gather.5.cloned.1.call-start = ((), (), s32[]{:S(2)}) async-start(), calls=%async_computation.2 | async-start | bytes 1769472 | tf_op jit(solution)/shard_map/all_gather | solution.py:31
  8.6 165.5 %reduce-scatter.3.cloned.1.call-start = ((), (), s32[]{:S(2)}) async-start(), calls=%async_computation.4 | async-start | bytes 13369344 | tf_op jit(solution)/shard_map/reduce_scatter | solution.py:39
  63.0 7.5 %copy-start = (bf16[1024,3072]{1,0:T(8,128)(2,1)S(1)}, bf16[1024,3072]{1,0:T(8,128)(2,1)}, u32[]{:S(2)}) copy-start(bf16[1024,3072]{1,0:T(8,128)(2,1)} %convolution_convert_fusion) | copy-start | bytes 18874372
  79.4 0.8 copy-start.1
  79.4 1.5 copy-start.2
  79.4 171.1 %all-gather.9.cloned.1.call-start = ((), (), s32[]{:S(2)}) async-start(), calls=%async_computation.5 | async-start | bytes 6684672 | tf_op jit(solution)/shard_map/all_gather | solution.py:52
  80.4 94.9 %copy-start.3 = (f32[3072]{0:T(1024)S(1)}, f32[3072]{0:T(1024)}, u32[]{:S(2)}) copy-start(f32[3072]{0:T(1024)} %param.11) | copy-start | bytes 36868
  176.6 124.0 %all-gather.11.cloned.1.call-start = ((), (), s32[]{:S(2)}) async-start(), calls=%async_computation.7 | async-start | bytes 6684672 | tf_op jit(solution)/shard_map/all_gather | solution.py:51
  177.2 158.9 %reduce-scatter.5.cloned.1.call-start = ((), (), s32[]{:S(2)}) async-start(), calls=%async_computation.6 | async-start | bytes 1769472 | tf_op jit(solution)/shard_map/reduce_scatter | solution.py:56
  250.5 9.6 %copy-start.5 = (bf16[1024,768]{1,0:T(8,128)(2,1)S(1)}, bf16[1024,768]{1,0:T(8,128)(2,1)}, u32[]{:S(2)}) copy-start(bf16[1024,768]{1,0:T(8,128)(2,1)} %all-gather.5.cloned.1.call-done) | copy-start | bytes 4718596
  269.9 30.7 %copy-start.4 = (bf16[1024,768]{1,0:T(8,128)(2,1)S(1)}, bf16[1024,768]{1,0:T(8,128)(2,1)}, u32[]{:S(2)}) copy-start(bf16[1024,768]{1,0:T(8,128)(2,1)} %all-gather.7.cloned.1.call-done) | copy-start | bytes 4718596
Sparse Core Ops, SparseCore 0:
  9.7 26.9 all-gather.6
  38.4 24.5 all-gather.4
  79.5 94.5 reduce-scatter.2
  176.7 60.9 all-gather.8
  239.7 60.7 all-gather.10
  303.4 32.6 reduce-scatter.4
where the time goes:
time: 343 us
  waiting for transfers between devices  189 us (55%)
  blocking collectives  72.6 us (21%)
  matrix products  45.7 us (13%)
  between operations  14.2 us (4%)
  other arithmetic  11.9 us (3%)
  local copies, waits for them, and re-layouts  8.94 us (3%)
    reduce_scatter x1, waiting for transfers between devices, body(): lax.psum_scatter(jnp.concatenate([pre_part, back_part], axis=1).astype(jn...  92.4 us
    psum x1, blocking collectives, body(): bias_total = lax.psum(bias_local, 'row')  72.6 us
    all_gather x1, waiting for transfers between devices, body(): lax.all_gather(grad_out, 'col', axis=0, tiled=True)  28 us
    reduce_scatter x1, waiting for transfers between devices, body(): lax.psum_scatter(contract_cols(grad_pre_all, up_weight).astype(jnp.bfloat...  25.8 us
    all_gather x1, waiting for transfers between devices, body(): lax.all_gather(hidden, 'row', axis=0, tiled=True)  23.9 us
    dot_general x2, matrix products, contract_rows(): lax.dot_general(left, right, (((0,), (0,)), ((), ())), preferred_element_...  19.4 us
    dot_general x2, matrix products, contract_cols(): lax.dot_general(left, right, (((1,), (1,)), ((), ())), preferred_element_...  18.8 us
    all_gather x1, waiting for transfers between devices, body(): lax.all_gather(tokens, 'col', axis=0, tiled=True)  17.1 us
  transfers between devices with their start and end apart: 6, of which 5 were waited for; matrix products, arithmetic and copies ran while one was open for 14% of the time, Pallas kernels for 0%

commit v1 on v0

v1 whole, which is shorter than its diff:
```python
import functools
import math

import jax
import jax.numpy as jnp
from jax import lax
from jax.experimental import pallas as pl
from jax.experimental.pallas import tpu as pltpu
from jax.sharding import PartitionSpec as P

MESH = pl.DeviceIdType.MESH
TOK = 1024
DB = 768
FB = 3072
WIDE = 256
HALF = 128
NJ = FB // WIDE
NP = 2 * NJ
SLOTS = 12
KEEP = 1.0 / 0.9
SCALE = 1.0 / math.sqrt(TOK)
BF = jnp.bfloat16
F32 = jnp.float32
LAG_B, LAG_C, LAG_D, LAG_E, LAG_F, LAG_G, LAG_H, LAG_M = 1, 2, 3, 4, 5, 6, 7, 8


def dot_nt(left, right):
    return lax.dot_general(left, right, (((1,), (1,)), ((), ())), preferred_element_type=F32)


def kernel(
    tok_hbm, grd_hbm, up_hbm, down_hbm, bias_ref, relu_ref, drop_ref,
    gt_out, gu_out, gd_out, gb_out,
    tok, grd, tok_t, up, down, keep, acc, cols,
    part, r1, r2, summed, t1, t2, full,
    st_up, st_down, gtp, gtr, z1, z2, st_gt,
    ss, rs, ag_s, ag_r, gt_s, gt_r, loc, out_sem,
):
    row = lax.axis_index("row")
    col = lax.axis_index("col")
    x, y, z, c = row // 4, row % 4, col // 2, col % 2

    def plus(v):
        return lax.rem(v + 1, 4)

    def minus(v):
        return lax.rem(v + 3, 4)

    def far(v):
        return lax.rem(v + 2, 4)

    xp, xm = (plus(x) * 4 + y, col), (minus(x) * 4 + y, col)
    yp, ym = (x * 4 + plus(y), col), (x * 4 + minus(y), col)
    zp, zm = (row, plus(z) * 2 + c), (row, minus(z) * 2 + c)
    sib = (row, z * 2 + (1 - c))
    everyone = (xp, xm, yp, ym, zp, zm, sib)

    def remote(src, dst, s, r, dev):
        return pltpu.make_async_remote_copy(
            src_ref=src, dst_ref=dst, send_sem=s, recv_sem=r, device_id=dev, device_id_type=MESH
        )

    loads = [
        pltpu.make_async_copy(grd_hbm, grd.at[pl.ds(pl.multiple_of(col * 128, 128), 128)], loc.at[0]),
        pltpu.make_async_copy(down_hbm.at[pl.ds(0, WIDE)], down.at[pl.ds(0, WIDE)], loc.at[1]),
        pltpu.make_async_copy(down_hbm.at[pl.ds(WIDE, FB - WIDE)], down.at[pl.ds(WIDE, FB - WIDE)], loc.at[2]),
        pltpu.make_async_copy(tok_hbm, tok.at[pl.ds(pl.multiple_of(col * 128, 128), 128)], loc.at[3]),
        pltpu.make_async_copy(up_hbm, up, loc.at[4]),
    ]
    for cp in loads:
        cp.start()

    barrier = pltpu.get_barrier_semaphore()
    for dev in everyone:
        pl.semaphore_signal(barrier, inc=1, device_id=dev, device_id_type=MESH)
    pl.semaphore_wait(barrier, len(everyone))

    def block_at(buf, zz, cc, lo=0, n=128):
        return buf.at[pl.ds(pl.multiple_of((zz * 2 + cc) * 128 + lo, 64), n)]

    def gather_copies(a, src, buf):
        s, r = ag_s.at[a], ag_r.at[a]
        mine = block_at(buf, z, c)
        below, above, opp = minus(z), plus(z), far(z)
        sends = [
            (src, mine, zp),
            (src, mine, zm),
            (src, mine, sib),
            (block_at(buf, below, c, 0, 64), block_at(buf, below, c, 0, 64), zp),
            (block_at(buf, above, c, 64, 64), block_at(buf, above, c, 64, 64), zm),
            (block_at(buf, below, c), block_at(buf, below, c), sib),
            (block_at(buf, above, c), block_at(buf, above, c), sib),
            (block_at(buf, opp, c), block_at(buf, opp, c), sib),
        ]
        o = 1 - c
        lands = [
            block_at(buf, below, c), block_at(buf, above, c), block_at(buf, z, o),
            block_at(buf, opp, c, 0, 64), block_at(buf, opp, c, 64, 64),
            block_at(buf, below, o), block_at(buf, above, o), block_at(buf, opp, o),
        ]

        def send(k):
            a, b, dev = sends[k]
            return remote(a, b, s.at[k], r.at[k], dev)

        def recv(k):
            return remote(lands[k], lands[k], s.at[k], r.at[k], zp)

        return send, recv

    def gather_0(a, src, buf):
        send, _ = gather_copies(a, src, buf)
        for k in (0, 1, 2):
            send(k).start()

    def gather_1(a, src, buf):
        send, recv = gather_copies(a, src, buf)
        recv(0).wait_recv()
        send(3).start()
        recv(1).wait_recv()
        send(4).start()
        send(5).start()
        send(6).start()

    def gather_2(a, src, buf):
        send, recv = gather_copies(a, src, buf)
        recv(3).wait_recv()
        recv(4).wait_recv()
        send(7).start()

    def gather_3(a, src, buf):
        send, recv = gather_copies(a, src, buf)
        for k in (2, 5, 6, 7):
            recv(k).wait_recv()
        for k in range(8):
            send(k).wait_send()

    gather_0(0, grd_hbm, grd)

    words = relu_ref[...] & drop_ref[...]
    low = (words & 255).astype(F32).astype(BF)
    high = (words >> 8).astype(F32).astype(BF)

    def unpack(j, carry):
        word = lax.broadcasted_iota(jnp.int32, (FB // 16, WIDE), 0)
        unit = lax.broadcasted_iota(jnp.int32, (FB // 16, WIDE), 1)
        spread = (word == j * (WIDE // 16) + unit // 16).astype(F32).astype(BF)
        lows = jnp.dot(low, spread, preferred_element_type=F32).astype(jnp.int32)
        highs = jnp.dot(high, spread, preferred_element_type=F32).astype(jnp.int32)
        bit = lax.broadcasted_iota(jnp.int32, (64, WIDE), 1) % 16
        picked = jnp.where(bit < 8, lows, highs)
        on = (picked >> (bit % 8)) & 1
        keep[:, pl.ds(pl.multiple_of(j * WIDE, WIDE), WIDE)] = on.astype(F32) * KEEP
        return carry

    lax.fori_loop(0, NJ, unpack, 0)
    acc[...] = jnp.zeros_like(acc)

    gather_1(0, grd_hbm, grd)
    gather_2(0, grd_hbm, grd)
    gather_3(0, grd_hbm, grd)
    loads[0].wait()
    loads[1].wait()

    flavours = ((x, y, xp, xm, yp, ym), (y, x, yp, ym, xp, xm))

    def piece(p, f):
        d1, d2, p1, m1, p2, m2 = flavours[f]
        w = lax.rem(p, SLOTS)
        s, r = ss.at[w, f], rs.at[w, f]
        pt, sm, g = part.at[w, f], summed.at[w, f], full.at[w, f]
        ra, rb, ta, tb = r1.at[w, f], r2.at[w, f], t1.at[w, f], t2.at[w, f]
        lo, hi = pl.ds(0, 2), pl.ds(2, 2)
        lo3, hi3 = pl.ds(0, 32), pl.ds(32, 32)
        n1, b1, o1 = plus(d1), minus(d1), far(d1)
        n2, b2, o2 = plus(d2), minus(d2), far(d2)
        sends = (
            (pt.at[o1, lo], ra.at[0], p1),
            (pt.at[o1, hi], ra.at[1], m1),
            (pt.at[n1, hi], rb.at[0, hi], p1),
            (pt.at[b1, lo], rb.at[1, lo], m1),
            (pt.at[n1, lo], rb.at[0, lo], p1),
            (pt.at[b1, hi], rb.at[1, hi], m1),
            (sm.at[o2, lo3], ta.at[0], p2),
            (sm.at[o2, hi3], ta.at[1], m2),
            (sm.at[n2, hi3], tb.at[0, hi3], p2),
            (sm.at[b2, lo3], tb.at[1, lo3], m2),
            (sm.at[n2, lo3], tb.at[0, lo3], p2),
            (sm.at[b2, hi3], tb.at[1, hi3], m2),
            (g.at[d1, d2], g.at[d1, d2], p2),
            (g.at[d1, d2], g.at[d1, d2], m2),
            (g.at[d1, b2, lo3], g.at[d1, b2, lo3], p2),
            (g.at[d1, n2, hi3], g.at[d1, n2, hi3], m2),
            (g.at[d1], g.at[d1], p1),
            (g.at[d1], g.at[d1], m1),
            (g.at[b1, lo], g.at[b1, lo], p1),
            (g.at[n1, hi], g.at[n1, hi], m1),
        )
        lands = (
            ra.at[0], ra.at[1], rb.at[0, hi], rb.at[1, lo], rb.at[0, lo], rb.at[1, hi],
            ta.at[0], ta.at[1], tb.at[0, hi3], tb.at[1, lo3], tb.at[0, lo3], tb.at[1, hi3],
            g.at[d1, b2], g.at[d1, n2], g.at[d1, o2, lo3], g.at[d1, o2, hi3],
            g.at[b1], g.at[n1], g.at[o1, lo], g.at[o1, hi],
        )

        def start(*ks):
            for k in ks:
                a, b, dev = sends[k]
                remote(a, b, s.at[k], r.at[k], dev).start()

        def landed(*ks):
            for k in ks:
                remote(lands[k], lands[k], s.at[k], r.at[k], p1).wait_recv()

        def sent(*ks):
            for k in ks:
                a, b, dev = sends[k]
                remote(a, b, s.at[k], r.at[k], dev).wait_send()

        return start, landed, sent

    def when_piece(i, lag):
        p = i - lag
        return p, (p >= 0) & (p < NP)

    def forward(p, left, weight):
        w = lax.rem(p, SLOTS)
        for q in range(4):
            res = weight(left[pl.ds(q * 256, 256), :]).astype(BF)
            part[w, 0, q] = res[:, :HALF].reshape(4, 64, HALF)
            for k in range(4):
                part[w, 1, k, q] = res[k * 64 : (k + 1) * 64, HALF:]

    def stage_a(p):
        w = lax.rem(p, SLOTS)

        @pl.when(p < NJ)
        def _():
            rows = down[pl.ds(pl.multiple_of(p * WIDE, WIDE), WIDE), :]
            forward(p, grd, lambda left: dot_nt(left, rows))

        @pl.when(p >= NJ)
        def _():
            lanes = up[:, pl.ds(pl.multiple_of((p - NJ) * WIDE, WIDE), WIDE)]
            forward(p, tok, lambda left: jnp.dot(left, lanes, preferred_element_type=F32))

        for f in range(2):
            start, _, _ = piece(p, f)
            start(0, 1, 2, 3)

    def stage_b(p):
        w = lax.rem(p, SLOTS)
        for f in range(2):
            d1 = flavours[f][0]
            start, landed, _ = piece(p, f)
            landed(0, 1)
            n1, b1 = plus(d1), minus(d1)
            part[w, f, n1, 0:2] = (part[w, f, n1, 0:2].astype(F32) + r1[w, f, 0].astype(F32)).astype(BF)
            part[w, f, b1, 2:4] = (part[w, f, b1, 2:4].astype(F32) + r1[w, f, 1].astype(F32)).astype(BF)
            start(4, 5)

    def stage_c(p):
        w = lax.rem(p, SLOTS)
        for f in range(2):
            d1 = flavours[f][0]
            start, landed, _ = piece(p, f)
            landed(2, 3, 4, 5)
            total = part[w, f, d1].astype(F32) + r2[w, f, 0].astype(F32) + r2[w, f, 1].astype(F32)
            summed[w, f] = total.astype(BF)
            start(6, 7, 8, 9)

    def stage_d(p):
        w = lax.rem(p, SLOTS)
        for f in range(2):
            d2 = flavours[f][1]
            start, landed, _ = piece(p, f)
            landed(6, 7)
            n2, b2 = plus(d2), minus(d2)
            summed[w, f, n2, 0:32] = (summed[w, f, n2, 0:32].astype(F32) + t1[w, f, 0].astype(F32)).astype(BF)
            summed[w, f, b2, 32:64] = (summed[w, f, b2, 32:64].astype(F32) + t1[w, f, 1].astype(F32)).astype(BF)
            start(10, 11)

    def stage_e(p):
        w = lax.rem(p, SLOTS)
        j = lax.rem(p, NJ)
        on_pre = (p >= NJ).astype(F32)
        for f in range(2):
            d1, d2 = flavours[f][:2]
            start, landed, sent = piece(p, f)
            landed(8, 9, 10, 11)
            total = summed[w, f, d2].astype(F32) + t2[w, f, 0].astype(F32) + t2[w, f, 1].astype(F32)
            lanes = pl.ds(pl.multiple_of(j * WIDE + f * HALF, HALF), HALF)
            total = total + bias_ref[0:1, lanes] * on_pre
            full[w, f, d1, d2] = (keep[:, lanes] * total).astype(BF)
            start(12, 13)
            sent(0, 1, 2, 3, 4, 5)

    def stage_f(p):
        for f in range(2):
            start, landed, _ = piece(p, f)
            landed(12, 13)
            start(14, 15)

    def stage_g(p):
        for f in range(2):
            start, landed, sent = piece(p, f)
            landed(14, 15)
            start(16, 17)
            sent(6, 7, 8, 9, 10, 11)

    def stage_h(p):
        for f in range(2):
            start, landed, _ = piece(p, f)
            landed(16, 17)
            start(18, 19)

    def store_up(j):
        w = lax.rem(j, 2)
        lanes = pl.ds(pl.multiple_of(j * WIDE, WIDE), WIDE)
        return pltpu.make_async_copy(st_up.at[w], gu_out.at[:, lanes], out_sem.at[w])

    def store_down(j):
        w = lax.rem(j, 2)
        rows = pl.ds(pl.multiple_of(j * WIDE, WIDE), WIDE)
        return pltpu.make_async_copy(st_down.at[w], gd_out.at[rows], out_sem.at[2 + w])

    def stage_m(p):
        w = lax.rem(p, SLOTS)
        for f in range(2):
            _, landed, _ = piece(p, f)
            landed(18, 19)
        cols[:, :HALF] = full[w, 0].reshape(TOK, HALF)
        for q in range(4):
            for k in range(4):
                cols[(q * 4 + k) * 64 : (q * 4 + k + 1) * 64, HALF:] = full[w, 1, k, q]

        @pl.when(p < NJ)
        def _():
            j = p
            lanes = pl.ds(pl.multiple_of(j * WIDE, WIDE), WIDE)

            @pl.when(j >= 2)
            def _():
                store_up(j).wait()

            for q in range(3):
                res = jnp.dot(tok_t[q * 256 : (q + 1) * 256, :], cols[...], preferred_element_type=F32)
                st_up[lax.rem(j, 2), q * 256 : (q + 1) * 256, :] = (res * SCALE).astype(BF)
            store_up(j).start()
            gb_out[0:1, lanes] = jnp.sum(cols[...].astype(F32), axis=0, keepdims=True) * SCALE
            for q in range(4):
                acc[q * 256 : (q + 1) * 256, :] += dot_nt(cols[q * 256 : (q + 1) * 256, :], up[:, lanes])

        @pl.when(p >= NJ)
        def _():
            j = p - NJ

            @pl.when(j >= 2)
            def _():
                store_down(j).wait()

            res = lax.dot_general(cols[...], grd[...], (((0,), (0,)), ((), ())), preferred_element_type=F32)
            st_down[lax.rem(j, 2)] = (res * SCALE).astype(BF)
            store_down(j).start()

        for f in range(2):
            _, _, sent = piece(p, f)
            sent(12, 13, 14, 15, 16, 17, 18, 19)

    def gt_copies():
        s, r = gt_s, gt_r
        mine = gtp.at[c]
        above, below, opp = plus(z), minus(z), far(z)
        lo, hi = pl.ds(0, 64), pl.ds(64, 64)
        sends = [
            (gtp.at[1 - c], gtr, sib),
            (mine.at[opp, lo], z1.at[0], zp),
            (mine.at[opp, hi], z1.at[1], zm),
            (mine.at[above, hi], z2.at[0, hi], zp),
            (mine.at[below, lo], z2.at[1, lo], zm),
            (mine.at[above, lo], z2.at[0, lo], zp),
            (mine.at[below, hi], z2.at[1, hi], zm),
        ]

        def send(k):
            a, b, dev = sends[k]
            return remote(a, b, s.at[k], r.at[k], dev)

        return send

    def gt_0():
        for q in range(8):
            gtp[q % 2, q // 2] = acc[q * 128 : (q + 1) * 128, :].astype(BF)
        gt_copies()(0).start()

    def gt_1():
        send = gt_copies()
        send(0).wait_recv()
        for q in range(4):
            gtp[c, q] = (gtp[c, q].astype(F32) + gtr[q].astype(F32)).astype(BF)
        for k in (1, 2, 3, 4):
            send(k).start()

    def gt_2():
        send = gt_copies()
        send(1).wait_recv()
        send(2).wait_recv()
        above, below = plus(z), minus(z)
        gtp[c, above, 0:64] = (gtp[c, above, 0:64].astype(F32) + z1[0].astype(F32)).astype(BF)
        gtp[c, below, 64:128] = (gtp[c, below, 64:128].astype(F32) + z1[1].astype(F32)).astype(BF)
        send(5).start()
        send(6).start()

    def gt_3():
        send = gt_copies()
        for k in (3, 4, 5, 6):
            send(k).wait_recv()
        st_gt[...] = (gtp[c, z].astype(F32) + z2[0].astype(F32) + z2[1].astype(F32)).astype(BF)
        cp = pltpu.make_async_copy(st_gt, gt_out, out_sem.at[4])
        cp.start()
        for k in range(7):
            send(k).wait_send()
        cp.wait()

    def step(i, carry):
        for fn, lag in (
            (stage_h, LAG_H), (stage_g, LAG_G), (stage_f, LAG_F), (stage_e, LAG_E),
            (stage_d, LAG_D), (stage_c, LAG_C), (stage_b, LAG_B), (stage_a, 0), (stage_m, LAG_M),
        ):
            p, on = when_piece(i, lag)
            pl.when(on)(functools.partial(fn, p))

        def at(n):
            return pl.when(i == n)

        @at(0)
        def _():
            loads[2].wait()
            gather_0(1, tok_hbm, tok)

        @at(2)
        def _():
            gather_1(1, tok_hbm, tok)

        @at(4)
        def _():
            gather_2(1, tok_hbm, tok)

        @at(6)
        def _():
            gather_3(1, tok_hbm, tok)
            loads[3].wait()
            loads[4].wait()
            for q in range(8):
                tok_t[:, q * 128 : (q + 1) * 128] = tok[q * 128 : (q + 1) * 128, :].T

        last = LAG_M + NJ - 1
        at(last)(gt_0)
        at(last + 2)(gt_1)
        at(last + 4)(gt_2)
        at(last + 7)(gt_3)
        return carry

    lax.fori_loop(0, NP + LAG_M, step, 0)
    for j in (NJ - 2, NJ - 1):
        store_up(j).wait()
        store_down(j).wait()


def body(tokens, grad_out, up_weight, down_weight, up_bias, relu_bits, drop_bits):
    hbm = pl.BlockSpec(memory_space=pl.ANY)
    vmem = pl.BlockSpec(memory_space=pltpu.VMEM)
    dma = pltpu.SemaphoreType.DMA
    gt, gu, gd, gb = pl.pallas_call(
        kernel,
        out_shape=(
            jax.ShapeDtypeStruct((128, DB), BF),
            jax.ShapeDtypeStruct((DB, FB), BF),
            jax.ShapeDtypeStruct((FB, DB), BF),
            jax.ShapeDtypeStruct((1, FB), F32),
        ),
        in_specs=[hbm, hbm, hbm, hbm, vmem, vmem, vmem],
        out_specs=(hbm, hbm, hbm, vmem),
        scratch_shapes=[
            pltpu.VMEM((TOK, DB), BF),
            pltpu.VMEM((TOK, DB), BF),
            pltpu.VMEM((DB, TOK), BF),
            pltpu.VMEM((DB, FB), BF),
            pltpu.VMEM((FB, DB), BF),
            pltpu.VMEM((64, FB), F32),
            pltpu.VMEM((TOK, DB), F32),
            pltpu.VMEM((TOK, WIDE), BF),
            pltpu.VMEM((SLOTS, 2, 4, 4, 64, HALF), BF),
            pltpu.VMEM((SLOTS, 2, 2, 2, 64, HALF), BF),
            pltpu.VMEM((SLOTS, 2, 2, 4, 64, HALF), BF),
            pltpu.VMEM((SLOTS, 2, 4, 64, HALF), BF),
            pltpu.VMEM((SLOTS, 2, 2, 32, HALF), BF),
            pltpu.VMEM((SLOTS, 2, 2, 64, HALF), BF),
            pltpu.VMEM((SLOTS, 2, 4, 4, 64, HALF), BF),
            pltpu.VMEM((2, DB, WIDE), BF),
            pltpu.VMEM((2, WIDE, DB), BF),
            pltpu.VMEM((2, 4, 128, DB), BF),
            pltpu.VMEM((4, 128, DB), BF),
            pltpu.VMEM((2, 64, DB), BF),
            pltpu.VMEM((2, 128, DB), BF),
            pltpu.VMEM((128, DB), BF),
            dma((SLOTS, 2, 20)),
            dma((SLOTS, 2, 20)),
            dma((2, 8)),
            dma((2, 8)),
            dma((7,)),
            dma((7,)),
            dma((5,)),
            dma((5,)),
        ],
        compiler_params=pltpu.CompilerParams(
            collective_id=0, has_side_effects=True, vmem_limit_bytes=60 * 2**20
        ),
        cost_estimate=pl.CostEstimate(
            flops=10 * TOK * DB * FB, bytes_accessed=10 * DB * FB, transcendentals=0
        ),
        name="fused",
    )(tokens, grad_out, up_weight, down_weight, up_bias.reshape(1, FB), relu_bits, drop_bits)
    return gt, gu, gd, gb.reshape(FB)


def solution(mesh):
    return jax.shard_map(
        body,
        mesh=mesh,
        in_specs=(
            P("col", "row"), P("col", "row"), P("row", "col"), P("col", "row"),
            P("col"), P("row", "col"), P("row", "col"),
        ),
        out_specs=(P("col", "row"), P("row", "col"), P("col", "row"), P("col")),
        check_vma=False,
    )
```

time: 343 us -> 189 us (0.55)
  waiting for transfers between devices: 189 us -> 0 us
  Pallas kernels: 0 us -> 179 us
  blocking collectives: 72.6 us -> 0 us
  matrix products: 45.7 us -> 0 us
  between operations: 14.2 us -> 0.66 us
  other arithmetic: 11.9 us -> 0.01 us
    pallas_call x0 -> x1, Pallas kernels: none -> 179 us  [body(): pl.pallas_call(kernel, out_shape=(jax.ShapeDtypeStruct((128, DB), BF), ja...]
    reduce_scatter x2 -> x0, waiting for transfers between devices: 118 us -> none  [the longest x1 92.4 us: body(): lax.psum_scatter(jnp.concatenate([pre_part, back_part], axis=1).astype(jn...]
    psum x1 -> x0, blocking collectives: 72.6 us -> none  [body(): bias_total = lax.psum(bias_local, 'row')]
    all_gather x4 -> x0, waiting for transfers between devices: 69.1 us -> none  [the longest x1 28 us: body(): lax.all_gather(grad_out, 'col', axis=0, tiled=True)]
    dot_general x5 -> x0, matrix products: 45.7 us -> none  [the longest x2 19.4 us: contract_rows(): lax.dot_general(left, right, (((0,), (0,)), ((), ())), preferred_element_...]
    concatenate x1 -> x0, other arithmetic: 8.82 us -> none  [body(): jnp.concatenate([pre_part, back_part], axis=1).astype(jnp.bfloat16)]
    unnamed x15 -> x10, local copies, waits for them, and re-layouts: 7.74 us -> 9.47 us
  transfers between devices with their start and end apart: 6 -> 0, of which waited for: 5 -> 0; matrix products, arithmetic and copies ran while one was open for 14% -> 0% of each run, Pallas kernels for 0% -> 0%
where the time goes in v1:
time: 189 us
  Pallas kernels  179 us (95%)
  local copies, waits for them, and re-layouts  9.47 us (5%)
    pallas_call x1, Pallas kernels, body(): pl.pallas_call(kernel, out_shape=(jax.ShapeDtypeStruct((128, DB), BF), ja...  179 us
    unnamed x10, local copies, waits for them, and re-layouts  9.47 us

profile of v1, /device:TPU:0, one launch (start us, length us, event | category | flops | bytes accessed | tf_op | source)
XLA Modules:
  0.0 189.0 jit_solution(8085249741456866820)
XLA Ops:
  0.6 178.8 %fused.1 = (bf16[128,768]{1,0:T(8,128)(2,1)}, bf16[768,3072]{1,0:T(8,128)(2,1)}, bf16[3072,768]{1,0:T(8,128)(2,1)}, f32[1,3072]{1,0:T(1,128)}) custom-call(bf16[128,768]{1,0:T(8,128)(2,1)} %tok_hbm.1, bf16[128,768]{1,0:T(8,128)(2,1)} %grd_hbm.1, bf16[768,3072]{1,0:T(8,128)(2,1)} %up_hbm.1, bf16[3072,768]{1,0:T(8,128)(2,1)} %down_hbm.1, f32[1,3072]{1,0:T(1,128)} %bitcast.5, ...), custom_call_target="tpu_custom_call" | custom-call | flops 24159191040 | bytes 23592960 | tf_op jit(solution)/shard_map/fused/pallas_call | solution.py:474
  179.5 0.0 slice-start
  179.5 1.8 copy.15
  181.3 0.0 slice-start.1
  181.3 4.9 %copy.16 = bf16[768,3072]{1,0:T(8,128)(2,1)} copy(bf16[768,3072]{1,0:T(8,128)(2,1)} %get-tuple-element.17) | data formatting | bytes 9437184
  186.2 0.0 slice-done
  186.2 0.0 slice-done.1
  186.2 0.0 copy-start
  186.2 2.2 %copy.17 = bf16[3072,768]{1,0:T(8,128)(2,1)} copy(bf16[3072,768]{1,0:T(8,128)(2,1)S(1)} %bitcast.3) | data formatting | bytes 9437184
  188.4 0.0 copy-done
  188.4 0.6 copy.18
  (1 shorter events, 0.0 us)
Async XLA Ops:
  179.5 6.7 %slice-start = ((s8[4718592]{0:T(1024)(128)(4,1)}), s8[4194304]{0:T(1024)(128)(4,1)S(1)}, s32[]{:S(2)}) async-start(s8[4718592]{0:T(1024)(128)(4,1)} %bitcast.2), calls=%async_computation | async-start | bytes 8388608
  181.3 4.9 %slice-start.1 = ((s8[4718592]{0:T(1024)(128)(4,1)}), s8[524288]{0:T(1024)(128)(4,1)S(1)}, s32[]{:S(2)}) async-start(s8[4718592]{0:T(1024)(128)(4,1)} %bitcast.2), calls=%async_computation.1 | async-start | bytes 1048576
  186.2 2.2 %copy-start = (f32[1,3072]{1,0:T(1,128)S(1)}, f32[1,3072]{1,0:T(1,128)}, u32[]{:S(2)}) copy-start(f32[1,3072]{1,0:T(1,128)} %get-tuple-element.11) | copy-start | bytes 36868

commit v2 on v1

v2 whole, which is shorter than its diff:
```python
import functools
import math

import jax
import jax.numpy as jnp
from jax import lax
from jax.experimental import pallas as pl
from jax.experimental.pallas import tpu as pltpu
from jax.sharding import PartitionSpec as P

MESH = pl.DeviceIdType.MESH
TOK = 1024
DB = 768
FB = 3072
WIDE = 256
HALF = 128
NJ = FB // WIDE
NP = 2 * NJ
RING = 16
HELD = 16
EARLY = 8
SLACK = 1
KEEP = 1.0 / 0.9
SCALE = 1.0 / math.sqrt(TOK)
BF = jnp.bfloat16
F32 = jnp.float32
GROUP = (0, 0, 1, 1, 1, 1, 2, 2, 3, 3, 3, 3, 4, 4, 5, 5, 6, 6, 7, 7)
LAG_A, LAG_B, LAG_C, LAG_D, LAG_E, LAG_F, LAG_G, LAG_H, LAG_M = -EARLY, 0, 2, 4, 6, 8, 10, 12, 14


def dot_nt(left, right):
    return lax.dot_general(left, right, (((1,), (1,)), ((), ())), preferred_element_type=F32)


def kernel(
    tok_hbm, grd_hbm, up_hbm, down_hbm, bias_hbm, relu_hbm, drop_hbm,
    gt_out, gu_out, gd_out, gb_out,
    tok, grd, tok_t, up, down, keep, acc, cols,
    part, r1, r2, summed, t1, t2, full,
    gtp, gtr, z1, z2, words, dropped, swapped, bias,
    ss, rs, ag_s, ag_r, gt_s, gt_r, sw_s, sw_r, pace, loc,
):
    row = lax.axis_index("row")
    col = lax.axis_index("col")
    x, y, z, c = row // 4, row % 4, col // 2, col % 2

    def plus(v):
        return lax.rem(v + 1, 4)

    def minus(v):
        return lax.rem(v + 3, 4)

    def far(v):
        return lax.rem(v + 2, 4)

    xp, xm = (plus(x) * 4 + y, col), (minus(x) * 4 + y, col)
    yp, ym = (x * 4 + plus(y), col), (x * 4 + minus(y), col)
    zp, zm = (row, plus(z) * 2 + c), (row, minus(z) * 2 + c)
    sib = (row, z * 2 + (1 - c))
    everyone = (xp, xm, yp, ym, zp, zm, sib)

    def remote(src, dst, s, r, dev):
        return pltpu.make_async_remote_copy(
            src_ref=src, dst_ref=dst, send_sem=s, recv_sem=r, device_id=dev, device_id_type=MESH
        )

    third = FB // 3
    loads = [
        pltpu.make_async_copy(grd_hbm, grd.at[pl.ds(pl.multiple_of(col * 128, 128), 128)], loc.at[0]),
        pltpu.make_async_copy(down_hbm.at[pl.ds(0, third)], down.at[pl.ds(0, third)], loc.at[1]),
        pltpu.make_async_copy(down_hbm.at[pl.ds(third, 2 * third)], down.at[pl.ds(third, 2 * third)], loc.at[2]),
        pltpu.make_async_copy(tok_hbm, tok.at[pl.ds(pl.multiple_of(col * 128, 128), 128)], loc.at[3]),
        pltpu.make_async_copy(up_hbm, up, loc.at[4]),
        pltpu.make_async_copy(relu_hbm, words, loc.at[5]),
        pltpu.make_async_copy(drop_hbm, dropped, loc.at[6]),
        pltpu.make_async_copy(bias_hbm, bias, loc.at[7]),
    ]
    for k in (0, 1, 5, 6):
        loads[k].start()

    barrier = pltpu.get_barrier_semaphore()
    for dev in everyone:
        pl.semaphore_signal(barrier, inc=1, device_id=dev, device_id_type=MESH)
    mirror = (y * 4 + x, col)

    @pl.when(x != y)
    def _():
        pl.semaphore_signal(barrier, inc=1, device_id=mirror, device_id_type=MESH)

    pl.semaphore_wait(barrier, len(everyone) + (x != y).astype(jnp.int32))

    def block_at(buf, zz, cc, lo=0, n=128):
        return buf.at[pl.ds(pl.multiple_of((zz * 2 + cc) * 128 + lo, 64), n)]

    def gather_copies(a, src, buf):
        s, r = ag_s.at[a], ag_r.at[a]
        mine = block_at(buf, z, c)
        below, above, opp = minus(z), plus(z), far(z)
        lower, upper = block_at(buf, z, c, 0, 64), block_at(buf, z, c, 64, 64)
        src_lower, src_upper = src.at[pl.ds(0, 64)], src.at[pl.ds(64, 64)]
        far_lower, far_upper = block_at(buf, opp, c, 0, 64), block_at(buf, opp, c, 64, 64)
        sends = [
            (src_lower, lower, zp),
            (src_upper, upper, zp),
            (src_upper, upper, zm),
            (src_lower, lower, zm),
            (src, mine, sib),
            (block_at(buf, below, c, 0, 64), block_at(buf, below, c, 0, 64), zp),
            (block_at(buf, above, c, 64, 64), block_at(buf, above, c, 64, 64), zm),
            (block_at(buf, below, c), block_at(buf, below, c), sib),
            (block_at(buf, above, c), block_at(buf, above, c), sib),
            (far_lower, far_lower, sib),
            (far_upper, far_upper, sib),
        ]
        o = 1 - c
        lands = [
            block_at(buf, below, c, 0, 64), block_at(buf, below, c, 64, 64),
            block_at(buf, above, c, 64, 64), block_at(buf, above, c, 0, 64),
            block_at(buf, z, o),
            far_lower, far_upper,
            block_at(buf, below, o), block_at(buf, above, o),
            block_at(buf, opp, o, 0, 64), block_at(buf, opp, o, 64, 64),
        ]

        def send(k):
            a, b, dev = sends[k]
            return remote(a, b, s.at[k], r.at[k], dev)

        def recv(k):
            return remote(lands[k], lands[k], s.at[k], r.at[k], zp)

        return send, recv

    def gather_0(a, src, buf):
        send, _ = gather_copies(a, src, buf)
        for k in (4, 0, 2, 1, 3):
            send(k).start()

    def gather_1(a, src, buf):
        send, recv = gather_copies(a, src, buf)
        for got, on in ((0, 5), (2, 6), (1, 7), (3, 8)):
            recv(got).wait_recv()
            send(on).start()

    def gather_2(a, src, buf):
        send, recv = gather_copies(a, src, buf)
        for got, on in ((5, 9), (6, 10)):
            recv(got).wait_recv()
            send(on).start()

    def gather_3(a, src, buf):
        send, recv = gather_copies(a, src, buf)
        for k in (4, 7, 8, 9, 10):
            recv(k).wait_recv()
        for k in range(11):
            send(k).wait_send()

    gather_0(0, grd_hbm, grd)
    for k in (2, 7):
        loads[k].start()

    swap = remote(words, swapped, sw_s, sw_r, mirror)
    loads[5].wait()
    loads[6].wait()
    words[...] = words[...] & dropped[...]

    @pl.when(x != y)
    def _():
        swap.start()

    @pl.when(x == y)
    def _():
        swapped[...] = words[...]

    def unpack(j):
        word = lax.broadcasted_iota(jnp.int32, (FB // 16, HALF), 0)
        unit = lax.broadcasted_iota(jnp.int32, (FB // 16, HALF), 1)
        bit = lax.broadcasted_iota(jnp.int32, (64, HALF), 1) % 16
        for f, ref in enumerate((swapped, words)):
            got = ref[...]
            low = (got & 255).astype(F32).astype(BF)
            high = (got >> 8).astype(F32).astype(BF)
            spread = (word == (j * WIDE + f * HALF + unit) // 16).astype(F32).astype(BF)
            lows = jnp.dot(low, spread, preferred_element_type=F32).astype(jnp.int32)
            highs = jnp.dot(high, spread, preferred_element_type=F32).astype(jnp.int32)
            picked = jnp.where(bit < 8, lows, highs)
            on = (picked >> (bit % 8)) & 1
            keep[:, pl.ds(pl.multiple_of(j * WIDE + f * HALF, HALF), HALF)] = on.astype(F32) * KEEP

    flavours = ((x, y, xp, xm, yp, ym), (y, x, yp, ym, xp, xm))

    def forward_block(p, left, weight, q):
        w = lax.rem(p, RING)
        res = weight(left[pl.ds(pl.multiple_of(q * 256, 256), 256), :]).astype(BF)
        for f in range(2):
            for k in range(4):
                part[w, f, k, q] = res[k * 64 : (k + 1) * 64, f * HALF : (f + 1) * HALF]

    def early(q, first=0, end=EARLY):
        top = q // 2

        def one(p, carry):
            rows = down[pl.ds(pl.multiple_of(p * WIDE, WIDE), WIDE), :]
            forward_block(p, grd, lambda left: dot_nt(left, rows), q)
            for f in range(2):
                d1 = flavours[f][0]
                pt, ra, rb, s, r = part.at[p, f], r1.at[p, f], r2.at[p, f], ss.at[p, f], rs.at[p, f]

                def along(off):
                    to = lax.rem(d1 + off, 4)
                    return to, ((to * 4 + y, col) if f == 0 else (x * 4 + to, col))

                _, dev = along(1 + 2 * top)
                remote(pt.at[far(d1), q], ra.at[top, q - 2 * top], s.at[0], r.at[0], dev).start()
                to, dev = along(3 - 2 * top)
                remote(pt.at[to, q], rb.at[1 - top, q], s.at[0], r.at[1], dev).start()
            return carry

        lax.fori_loop(first, end, one, 0)

    loads[0].wait()
    loads[1].wait()
    send, recv = gather_copies(0, grd_hbm, grd)
    recv(4).wait_recv()
    early(z, 0, EARLY // 2)
    for got, on in ((0, 5), (2, 6)):
        recv(got).wait_recv()
        send(on).start()
    loads[2].wait()
    early(z, EARLY // 2, EARLY)
    for got, on in ((1, 7), (3, 8)):
        recv(got).wait_recv()
        send(on).start()
    gather_0(1, tok_hbm, tok)
    loads[3].start()
    loads[4].start()
    recv(7).wait_recv()
    early(minus(z))
    for got, on in ((5, 9), (6, 10)):
        recv(got).wait_recv()
        send(on).start()
    recv(8).wait_recv()
    early(plus(z))
    for k in (9, 10):
        recv(k).wait_recv()
    early(far(z))
    for k in range(11):
        send(k).wait_send()
    loads[7].wait()

    def piece(p, f):
        d1, d2, p1, m1, p2, m2 = flavours[f]
        w, v = lax.rem(p, RING), lax.rem(p, HELD)
        s, r = ss.at[v, f], rs.at[v, f]
        pt, sm, g = part.at[w, f], summed.at[w, f], full.at[v, f]
        ra, rb, ta, tb = r1.at[w, f], r2.at[w, f], t1.at[w, f], t2.at[w, f]
        lo, hi = pl.ds(0, 2), pl.ds(2, 2)
        lo3, hi3 = pl.ds(0, 32), pl.ds(32, 32)
        n1, b1, o1 = plus(d1), minus(d1), far(d1)
        n2, b2, o2 = plus(d2), minus(d2), far(d2)
        sends = (
            (pt.at[o1, lo], ra.at[0], p1),
            (pt.at[o1, hi], ra.at[1], m1),
            (pt.at[n1, hi], rb.at[0, hi], p1),
            (pt.at[b1, lo], rb.at[1, lo], m1),
            (pt.at[n1, lo], rb.at[0, lo], p1),
            (pt.at[b1, hi], rb.at[1, hi], m1),
            (sm.at[o2, lo3], ta.at[0], p2),
            (sm.at[o2, hi3], ta.at[1], m2),
            (sm.at[n2, hi3], tb.at[0, hi3], p2),
            (sm.at[b2, lo3], tb.at[1, lo3], m2),
            (sm.at[n2, lo3], tb.at[0, lo3], p2),
            (sm.at[b2, hi3], tb.at[1, hi3], m2),
            (g.at[d1, d2], g.at[d1, d2], p2),
            (g.at[d1, d2], g.at[d1, d2], m2),
            (g.at[d1, b2, lo3], g.at[d1, b2, lo3], p2),
            (g.at[d1, n2, hi3], g.at[d1, n2, hi3], m2),
            (g.at[d1], g.at[d1], p1),
            (g.at[d1], g.at[d1], m1),
            (g.at[b1, lo], g.at[b1, lo], p1),
            (g.at[n1, hi], g.at[n1, hi], m1),
        )
        lands = (ra, rb, ta, tb, g.at[o1, lo], g.at[d1, o2], g.at[pl.ds(0, 2)], g.at[o1])

        def start(*ks):
            for k in ks:
                a, b, dev = sends[k]
                remote(a, b, s.at[min(k // 6, 2)], r.at[GROUP[k]], dev).start()

        def landed(n):
            remote(lands[n], lands[n], s.at[0], r.at[n], p1).wait_recv()

        def sent(n):
            some = grd.at[pl.ds(0, (128, 32, 160)[n])]
            remote(some, some, s.at[n], r.at[0], p1).wait_send()

        return start, landed, sent

    def when_piece(i, lag):
        p = i - lag
        return p, (p >= 0) & (p < NP)

    def forward(p, left, weight):
        for q in range(4):
            forward_block(p, left, weight, q)

    def stage_a(p):

        @pl.when(p < NJ)
        def _():
            rows = down[pl.ds(pl.multiple_of(p * WIDE, WIDE), WIDE), :]
            forward(p, grd, lambda left: dot_nt(left, rows))

        @pl.when(p >= NJ)
        def _():
            lanes = up[:, pl.ds(pl.multiple_of((p - NJ) * WIDE, WIDE), WIDE)]
            forward(p, tok, lambda left: jnp.dot(left, lanes, preferred_element_type=F32))

        for f in range(2):
            start, _, _ = piece(p, f)
            start(0, 1, 2, 3)

    def stage_b(p):
        w = lax.rem(p, RING)
        for f in range(2):
            d1 = flavours[f][0]
            start, landed, _ = piece(p, f)
            landed(0)
            n1, b1 = plus(d1), minus(d1)
            part[w, f, n1, 0:2] = (part[w, f, n1, 0:2].astype(F32) + r1[w, f, 0].astype(F32)).astype(BF)
            part[w, f, b1, 2:4] = (part[w, f, b1, 2:4].astype(F32) + r1[w, f, 1].astype(F32)).astype(BF)
            start(4, 5)

    def stage_c(p):
        w = lax.rem(p, RING)
        for f in range(2):
            d1 = flavours[f][0]
            start, landed, _ = piece(p, f)
            landed(1)
            total = part[w, f, d1].astype(F32) + r2[w, f, 0].astype(F32) + r2[w, f, 1].astype(F32)
            summed[w, f] = total.astype(BF)
            start(6, 7, 8, 9)

    def stage_d(p):
        w = lax.rem(p, RING)
        for f in range(2):
            d2 = flavours[f][1]
            start, landed, _ = piece(p, f)
            landed(2)
            n2, b2 = plus(d2), minus(d2)
            summed[w, f, n2, 0:32] = (summed[w, f, n2, 0:32].astype(F32) + t1[w, f, 0].astype(F32)).astype(BF)
            summed[w, f, b2, 32:64] = (summed[w, f, b2, 32:64].astype(F32) + t1[w, f, 1].astype(F32)).astype(BF)
            start(10, 11)

    def stage_e(p):
        w, v = lax.rem(p, RING), lax.rem(p, HELD)
        j = lax.rem(p, NJ)
        on_pre = (p >= NJ).astype(F32)
        for f in range(2):
            d1, d2 = flavours[f][:2]
            start, landed, sent = piece(p, f)
            landed(3)
            total = summed[w, f, d2].astype(F32) + t2[w, f, 0].astype(F32) + t2[w, f, 1].astype(F32)
            lanes = pl.ds(pl.multiple_of(j * WIDE + f * HALF, HALF), HALF)
            total = total + bias[0:1, lanes] * on_pre
            full[v, f, d1, d2] = (keep[:, lanes] * total).astype(BF)
            start(12, 13)
            sent(0)

    def stage_f(p):
        for f in range(2):
            start, landed, _ = piece(p, f)
            landed(4)
            start(14, 15)

    def stage_g(p):
        for f in range(2):
            start, landed, sent = piece(p, f)
            landed(5)
            start(16, 17)
            sent(1)

    def stage_h(p):
        for f in range(2):
            start, landed, _ = piece(p, f)
            landed(6)
            start(18, 19)

    def stage_m(p):
        w = lax.rem(p, HELD)
        for f in range(2):
            _, landed, _ = piece(p, f)
            landed(7)
        for f in range(2):
            for q in range(4):
                for k in range(4):
                    cols[(q * 4 + k) * 64 : (q * 4 + k + 1) * 64, f * HALF : (f + 1) * HALF] = full[w, f, k, q]

        @pl.when(p < NJ)
        def _():
            j = p
            lanes = pl.ds(pl.multiple_of(j * WIDE, WIDE), WIDE)

            for q in range(3):
                res = jnp.dot(tok_t[q * 256 : (q + 1) * 256, :], cols[...], preferred_element_type=F32)
                gu_out[q * 256 : (q + 1) * 256, lanes] = (res * SCALE).astype(BF)
            gb_out[0:1, lanes] = jnp.sum(cols[...].astype(F32), axis=0, keepdims=True) * SCALE
            for q in range(4):
                acc[q * 256 : (q + 1) * 256, :] += dot_nt(cols[q * 256 : (q + 1) * 256, :], up[:, lanes])

        @pl.when(p >= NJ)
        def _():
            j = p - NJ

            res = lax.dot_general(cols[...], grd[...], (((0,), (0,)), ((), ())), preferred_element_type=F32)
            gd_out[pl.ds(pl.multiple_of(j * WIDE, WIDE), WIDE), :] = (res * SCALE).astype(BF)

        for f in range(2):
            _, _, sent = piece(p, f)
            sent(2)

    def gt_copies():
        s, r = gt_s, gt_r
        mine = gtp.at[c]
        above, below, opp = plus(z), minus(z), far(z)
        lo, hi = pl.ds(0, 64), pl.ds(64, 64)
        sends = [
            (gtp.at[1 - c], gtr, sib),
            (mine.at[opp, lo], z1.at[0], zp),
            (mine.at[opp, hi], z1.at[1], zm),
            (mine.at[above, hi], z2.at[0, hi], zp),
            (mine.at[below, lo], z2.at[1, lo], zm),
            (mine.at[above, lo], z2.at[0, lo], zp),
            (mine.at[below, hi], z2.at[1, hi], zm),
        ]

        def send(k):
            a, b, dev = sends[k]
            return remote(a, b, s.at[k], r.at[k], dev)

        return send

    def gt_0():
        for q in range(8):
            gtp[q % 2, q // 2] = acc[q * 128 : (q + 1) * 128, :].astype(BF)
        gt_copies()(0).start()

    def gt_1():
        send = gt_copies()
        send(0).wait_recv()
        for q in range(4):
            gtp[c, q] = (gtp[c, q].astype(F32) + gtr[q].astype(F32)).astype(BF)
        for k in (1, 2, 3, 4):
            send(k).start()

    def gt_2():
        send = gt_copies()
        send(1).wait_recv()
        send(2).wait_recv()
        above, below = plus(z), minus(z)
        gtp[c, above, 0:64] = (gtp[c, above, 0:64].astype(F32) + z1[0].astype(F32)).astype(BF)
        gtp[c, below, 64:128] = (gtp[c, below, 64:128].astype(F32) + z1[1].astype(F32)).astype(BF)
        send(5).start()
        send(6).start()

    def gt_3():
        send = gt_copies()
        for k in (3, 4, 5, 6):
            send(k).wait_recv()
        gt_out[...] = (gtp[c, z].astype(F32) + z2[0].astype(F32) + z2[1].astype(F32)).astype(BF)
        for k in range(7):
            send(k).wait_send()

    def step(i, carry):
        @pl.when(i >= SLACK)
        def _():
            pl.semaphore_wait(pace, 1)

        for fn, lag in (
            (stage_h, LAG_H), (stage_g, LAG_G), (stage_f, LAG_F), (stage_e, LAG_E),
            (stage_d, LAG_D), (stage_c, LAG_C), (stage_b, LAG_B), (stage_a, LAG_A), (stage_m, LAG_M),
        ):
            p, on = when_piece(i, lag)
            on = on & (p >= EARLY) if fn is stage_a else on
            pl.when(on)(functools.partial(fn, p))

        def at(n):
            return pl.when(i == n)

        @pl.when((i == 0) & (x != y))
        def _():
            swap.wait()

        pl.when(i < NJ)(functools.partial(unpack, i))

        @at(0)
        def _():
            gather_1(1, tok_hbm, tok)
            acc[...] = jnp.zeros_like(acc)

        @at(2)
        def _():
            gather_2(1, tok_hbm, tok)
            loads[3].wait()
            loads[4].wait()

        @at(3)
        def _():
            gather_3(1, tok_hbm, tok)

        @at(6)
        def _():
            for q in range(8):
                tok_t[:, q * 128 : (q + 1) * 128] = tok[q * 128 : (q + 1) * 128, :].T

        last = LAG_M + NJ - 1
        at(last)(gt_0)
        at(last + 2)(gt_1)
        at(last + 4)(gt_2)
        at(last + 7)(gt_3)
        pl.semaphore_signal(pace, inc=1, device_id=sib, device_id_type=MESH)
        return carry

    lax.fori_loop(0, NP + LAG_M, step, 0)
    pl.semaphore_wait(pace, SLACK)


def flush(gt, gu, gd, gb, gt_out, gu_out, gd_out, gb_out, sem):
    copies = [pltpu.make_async_copy(gt, gt_out, sem.at[0]), pltpu.make_async_copy(gb, gb_out, sem.at[1])]
    for q in range(4):
        rows = pl.ds(q * DB // 4, DB // 4)
        copies.append(pltpu.make_async_copy(gu.at[rows], gu_out.at[rows], sem.at[2 + q]))
        rows = pl.ds(q * FB // 4, FB // 4)
        copies.append(pltpu.make_async_copy(gd.at[rows], gd_out.at[rows], sem.at[6 + q]))
    for cp in copies:
        cp.start()
    for cp in copies:
        cp.wait()


def body(tokens, grad_out, up_weight, down_weight, up_bias, relu_bits, drop_bits):
    hbm = pl.BlockSpec(memory_space=pl.ANY)
    vmem = pl.BlockSpec(memory_space=pltpu.VMEM)
    dma = pltpu.SemaphoreType.DMA
    shapes = (((128, DB), BF), ((DB, FB), BF), ((FB, DB), BF), ((1, FB), F32))
    held = pl.pallas_call(
        kernel,
        out_shape=tuple(pltpu.VMEM(shape, dtype) for shape, dtype in shapes),
        in_specs=[hbm] * 7,
        out_specs=(vmem,) * 4,
        scratch_shapes=[
            pltpu.VMEM((TOK, DB), BF),
            pltpu.VMEM((TOK, DB), BF),
            pltpu.VMEM((DB, TOK), BF),
            pltpu.VMEM((DB, FB), BF),
            pltpu.VMEM((FB, DB), BF),
            pltpu.VMEM((64, FB), F32),
            pltpu.VMEM((TOK, DB), F32),
            pltpu.VMEM((TOK, WIDE), BF),
            pltpu.VMEM((RING, 2, 4, 4, 64, HALF), BF),
            pltpu.VMEM((RING, 2, 2, 2, 64, HALF), BF),
            pltpu.VMEM((RING, 2, 2, 4, 64, HALF), BF),
            pltpu.VMEM((RING, 2, 4, 64, HALF), BF),
            pltpu.VMEM((RING, 2, 2, 32, HALF), BF),
            pltpu.VMEM((RING, 2, 2, 64, HALF), BF),
            pltpu.VMEM((HELD, 2, 4, 4, 64, HALF), BF),
            pltpu.VMEM((2, 4, 128, DB), BF),
            pltpu.VMEM((4, 128, DB), BF),
            pltpu.VMEM((2, 64, DB), BF),
            pltpu.VMEM((2, 128, DB), BF),
            pltpu.VMEM((64, FB // 16), jnp.int32),
            pltpu.VMEM((64, FB // 16), jnp.int32),
            pltpu.VMEM((64, FB // 16), jnp.int32),
            pltpu.VMEM((1, FB), F32),
            dma((HELD, 2, 3)),
            dma((HELD, 2, 8)),
            dma((2, 11)),
            dma((2, 11)),
            dma((7,)),
            dma((7,)),
            dma,
            dma,
            pltpu.SemaphoreType.REGULAR,
            dma((8,)),
        ],
        compiler_params=pltpu.CompilerParams(
            collective_id=0, has_side_effects=True, vmem_limit_bytes=48 * 2**20
        ),
        cost_estimate=pl.CostEstimate(
            flops=10 * TOK * DB * FB, bytes_accessed=10 * DB * FB, transcendentals=0
        ),
        name="fused",
    )(tokens, grad_out, up_weight, down_weight, up_bias.reshape(1, FB), relu_bits, drop_bits)
    gt, gu, gd, gb = pl.pallas_call(
        flush,
        out_shape=tuple(jax.ShapeDtypeStruct(shape, dtype) for shape, dtype in shapes),
        in_specs=[vmem] * 4,
        out_specs=(hbm,) * 4,
        scratch_shapes=[dma((10,))],
        compiler_params=pltpu.CompilerParams(vmem_limit_bytes=2**20),
        name="flush",
    )(*held)
    return gt, gu, gd, gb.reshape(FB)


def solution(mesh):
    return jax.shard_map(
        body,
        mesh=mesh,
        in_specs=(
            P("col", "row"), P("col", "row"), P("row", "col"), P("col", "row"),
            P("col"), P("row", "col"), P("row", "col"),
        ),
        out_specs=(P("col", "row"), P("row", "col"), P("col", "row"), P("col")),
        check_vma=False,
    )
```

time: 189 us -> 155 us (0.82)
  Pallas kernels: 179 us -> 153 us
  local copies, waits for them, and re-layouts: 9.47 us -> 0 us
    pallas_call x1 -> x2, Pallas kernels: 179 us -> 153 us  [the longest x1 149 us: body(): pl.pallas_call(kernel, out_shape=tuple((pltpu.VMEM(shape, dtype) for shap...]
    unnamed x10 -> x0, local copies, waits for them, and re-layouts: 9.47 us -> none
where the time goes in v2:
time: 155 us; the launch traced here: 153 us
  Pallas kernels  153 us (99%)
    pallas_call x1, Pallas kernels, body(): pl.pallas_call(kernel, out_shape=tuple((pltpu.VMEM(shape, dtype) for shap...  149 us
    pallas_call x1, Pallas kernels, body(): pl.pallas_call(flush, out_shape=tuple((jax.ShapeDtypeStruct(shape, dtype)...  3.79 us

profile of v2, /device:TPU:0, one launch (start us, length us, event | category | flops | bytes accessed | tf_op | source)
XLA Modules:
  0.0 153.5 jit_solution(3522910520144286265)
XLA Ops:
  0.6 149.0 %fused.1 = (bf16[128,768]{1,0:T(8,128)(2,1)S(1)}, bf16[768,3072]{1,0:T(8,128)(2,1)S(1)}, bf16[3072,768]{1,0:T(8,128)(2,1)S(1)}, f32[1,3072]{1,0:T(1,128)S(1)}) custom-call(bf16[128,768]{1,0:T(8,128)(2,1)} %tok_hbm.1, bf16[128,768]{1,0:T(8,128)(2,1)} %grd_hbm.1, bf16[768,3072]{1,0:T(8,128)(2,1)} %up_hbm.1, bf16[3072,768]{1,0:T(8,128)(2,1)} %down_hbm.1, ...), custom_call_target="tpu_custom_call" | custom-call | flops 24159191040 | bytes 23592960 | tf_op jit(solution)/shard_map/fused/pallas_call | solution.py:546
  149.7 3.8 %flush.1 = (bf16[128,768]{1,0:T(8,128)(2,1)}, bf16[768,3072]{1,0:T(8,128)(2,1)}, bf16[3072,768]{1,0:T(8,128)(2,1)}, f32[1,3072]{1,0:T(1,128)}) custom-call(bf16[128,768]{1,0:T(8,128)(2,1)S(1)} %get-tuple-element.12.gt, bf16[768,3072]{1,0:T(8,128)(2,1)S(1)} %get-tuple-element.13.gu, bf16[3072,768]{1,0:T(8,128)(2,1)S(1)} %get-tuple-element.14.gd, ...), custom_call_target="tpu_custom_call" | custom-call | tf_op jit(solution)/shard_map/flush/pallas_call | solution.py:594

commit v3 on v2

--- a/solution.py
+++ b/solution.py
@@ -19,12 +19,14 @@
 RING = 16
 HELD = 16
 EARLY = 8
-SLACK = 1
 KEEP = 1.0 / 0.9
 SCALE = 1.0 / math.sqrt(TOK)
 BF = jnp.bfloat16
 F32 = jnp.float32
 GROUP = (0, 0, 1, 1, 1, 1, 2, 2, 3, 3, 3, 3, 4, 4, 5, 5, 6, 6, 7, 7)
+RECV_RING = ((0, 12), (12, 12), (24, 6), (30, 6), (36, 6), (42, 6), (48, 6), (54, 6))
+SEND_RING = ((0, 12), (12, 6), (18, 12))
+N_RECV, N_SEND = 60, 30
 LAG_A, LAG_B, LAG_C, LAG_D, LAG_E, LAG_F, LAG_G, LAG_H, LAG_M = -EARLY, 0, 2, 4, 6, 8, 10, 12, 14
 
 
@@ -38,7 +40,7 @@
     tok, grd, tok_t, up, down, keep, acc, cols,
     part, r1, r2, summed, t1, t2, full,
     gtp, gtr, z1, z2, words, dropped, swapped, bias,
-    ss, rs, ag_s, ag_r, gt_s, gt_r, sw_s, sw_r, pace, loc,
+    ss, rs, ag_s, ag_r, gt_s, gt_r, sw_s, sw_r, loc,
 ):
     row = lax.axis_index("row")
     col = lax.axis_index("col")
@@ -124,12 +126,16 @@
 
         def send(k):
             a, b, dev = sends[k]
-            return remote(a, b, s.at[k], r.at[k], dev)
+            return remote(a, b, s, r.at[k], dev)
 
         def recv(k):
-            return remote(lands[k], lands[k], s.at[k], r.at[k], zp)
+            return remote(lands[k], lands[k], s, r.at[k], zp)
 
         return send, recv
+
+    def all_sent(a, buf):
+        size = buf.at[pl.ds(0, 896)]
+        remote(size, size, ag_s.at[a], ag_r.at[a, 0], zp).wait_send()
 
     def gather_0(a, src, buf):
         send, _ = gather_copies(a, src, buf)
@@ -152,8 +158,7 @@
         send, recv = gather_copies(a, src, buf)
         for k in (4, 7, 8, 9, 10):
             recv(k).wait_recv()
-        for k in range(11):
-            send(k).wait_send()
+        all_sent(a, buf)
 
     gather_0(0, grd_hbm, grd)
     for k in (2, 7):
@@ -189,6 +194,14 @@
 
     flavours = ((x, y, xp, xm, yp, ym), (y, x, yp, ym, xp, xm))
 
+    def send_sem(p, n):
+        first, length = SEND_RING[n]
+        return ss.at[first + lax.rem(p, length)]
+
+    def recv_sem(p, n):
+        first, length = RECV_RING[n]
+        return rs.at[first + lax.rem(p, length)]
+
     def forward_block(p, left, weight, q):
         w = lax.rem(p, RING)
         res = weight(left[pl.ds(pl.multiple_of(q * 256, 256), 256), :]).astype(BF)
@@ -196,7 +209,7 @@
             for k in range(4):
                 part[w, f, k, q] = res[k * 64 : (k + 1) * 64, f * HALF : (f + 1) * HALF]
 
-    def early(q, first=0, end=EARLY):
+    def early(q, first, end):
         top = q // 2
 
         def one(p, carry):
@@ -204,54 +217,71 @@
             forward_block(p, grd, lambda left: dot_nt(left, rows), q)
             for f in range(2):
                 d1 = flavours[f][0]
-                pt, ra, rb, s, r = part.at[p, f], r1.at[p, f], r2.at[p, f], ss.at[p, f], rs.at[p, f]
+                pt, ra, rb = part.at[p, f], r1.at[p, f], r2.at[p, f]
 
                 def along(off):
                     to = lax.rem(d1 + off, 4)
                     return to, ((to * 4 + y, col) if f == 0 else (x * 4 + to, col))
 
                 _, dev = along(1 + 2 * top)
-                remote(pt.at[far(d1), q], ra.at[top, q - 2 * top], s.at[0], r.at[0], dev).start()
+                remote(pt.at[far(d1), q], ra.at[top, q - 2 * top], send_sem(p, 0), recv_sem(p, 0), dev).start()
                 to, dev = along(3 - 2 * top)
-                remote(pt.at[to, q], rb.at[1 - top, q], s.at[0], r.at[1], dev).start()
+                remote(pt.at[to, q], rb.at[1 - top, q], send_sem(p, 0), recv_sem(p, 1), dev).start()
             return carry
 
         lax.fori_loop(first, end, one, 0)
 
     loads[0].wait()
     loads[1].wait()
-    send, recv = gather_copies(0, grd_hbm, grd)
-    recv(4).wait_recv()
-    early(z, 0, EARLY // 2)
-    for got, on in ((0, 5), (2, 6)):
-        recv(got).wait_recv()
-        send(on).start()
-    loads[2].wait()
-    early(z, EARLY // 2, EARLY)
-    for got, on in ((1, 7), (3, 8)):
-        recv(got).wait_recv()
-        send(on).start()
-    gather_0(1, tok_hbm, tok)
-    loads[3].start()
-    loads[4].start()
-    recv(7).wait_recv()
-    early(minus(z))
-    for got, on in ((5, 9), (6, 10)):
-        recv(got).wait_recv()
-        send(on).start()
-    recv(8).wait_recv()
-    early(plus(z))
-    for k in (9, 10):
-        recv(k).wait_recv()
-    early(far(z))
-    for k in range(11):
-        send(k).wait_send()
+
+    def arrive(t, carry):
+        send, recv = gather_copies(0, grd_hbm, grd)
+
+        def forward_on(*pairs):
+            for got, on in pairs:
+                recv(got).wait_recv()
+                send(on).start()
+
+        @pl.when(t == 0)
+        def _():
+            recv(4).wait_recv()
+
+        @pl.when(t == 1)
+        def _():
+            forward_on((0, 5), (2, 6))
+            loads[2].wait()
+
+        @pl.when(t == 2)
+        def _():
+            forward_on((1, 7), (3, 8))
+            gather_0(1, tok_hbm, tok)
+            loads[3].start()
+            loads[4].start()
+            recv(8).wait_recv()
+
+        @pl.when(t == 3)
+        def _():
+            forward_on((5, 9), (6, 10))
+            recv(7).wait_recv()
+
+        @pl.when(t == 4)
+        def _():
+            for k in (9, 10):
+                recv(k).wait_recv()
+
+        u = (t * 4) // 5
+        first = (t == 1).astype(jnp.int32) * (EARLY // 2)
+        end = EARLY - (t == 0).astype(jnp.int32) * (EARLY - EARLY // 2)
+        early(lax.rem(z + u + u // 2 - 2 * (u // 3), 4), first, end)
+        return carry
+
+    lax.fori_loop(0, 5, arrive, 0)
+    all_sent(0, grd)
     loads[7].wait()
 
     def piece(p, f):
         d1, d2, p1, m1, p2, m2 = flavours[f]
         w, v = lax.rem(p, RING), lax.rem(p, HELD)
-        s, r = ss.at[v, f], rs.at[v, f]
         pt, sm, g = part.at[w, f], summed.at[w, f], full.at[v, f]
         ra, rb, ta, tb = r1.at[w, f], r2.at[w, f], t1.at[w, f], t2.at[w, f]
         lo, hi = pl.ds(0, 2), pl.ds(2, 2)
@@ -280,21 +310,23 @@
             (g.at[b1, lo], g.at[b1, lo], p1),
             (g.at[n1, hi], g.at[n1, hi], m1),
         )
-        lands = (ra, rb, ta, tb, g.at[o1, lo], g.at[d1, o2], g.at[pl.ds(0, 2)], g.at[o1])
 
         def start(*ks):
             for k in ks:
                 a, b, dev = sends[k]
-                remote(a, b, s.at[min(k // 6, 2)], r.at[GROUP[k]], dev).start()
-
-        def landed(n):
-            remote(lands[n], lands[n], s.at[0], r.at[n], p1).wait_recv()
-
-        def sent(n):
-            some = grd.at[pl.ds(0, (128, 32, 160)[n])]
-            remote(some, some, s.at[n], r.at[0], p1).wait_send()
-
-        return start, landed, sent
+                remote(a, b, send_sem(p, min(k // 6, 2)), recv_sem(p, GROUP[k]), dev).start()
+
+        return start
+
+    def landed(p, n):
+        w, v = lax.rem(p, RING), lax.rem(p, HELD)
+        g = full.at[v, 0]
+        size = (r1.at[w], r2.at[w], t1.at[w], t2.at[w], g.at[0], g.at[0, pl.ds(0, 2)], g, g.at[pl.ds(0, 2)])[n]
+        remote(size, size, send_sem(p, 0), recv_sem(p, n), xp).wait_recv()
+
+    def sent(p, n):
+        size = grd.at[pl.ds(0, (256, 64, 320)[n])]
+        remote(size, size, send_sem(p, n), recv_sem(p, 0), xp).wait_send()
 
     def when_piece(i, lag):
         p = i - lag
@@ -317,15 +349,15 @@
             forward(p, tok, lambda left: jnp.dot(left, lanes, preferred_element_type=F32))
 
         for f in range(2):
-            start, _, _ = piece(p, f)
+            start = piece(p, f)
             start(0, 1, 2, 3)
 
     def stage_b(p):
         w = lax.rem(p, RING)
+        landed(p, 0)
         for f in range(2):
             d1 = flavours[f][0]
-            start, landed, _ = piece(p, f)
-            landed(0)
+            start = piece(p, f)
             n1, b1 = plus(d1), minus(d1)
             part[w, f, n1, 0:2] = (part[w, f, n1, 0:2].astype(F32) + r1[w, f, 0].astype(F32)).astype(BF)
             part[w, f, b1, 2:4] = (part[w, f, b1, 2:4].astype(F32) + r1[w, f, 1].astype(F32)).astype(BF)
@@ -333,20 +365,21 @@
 
     def stage_c(p):
         w = lax.rem(p, RING)
+        landed(p, 1)
         for f in range(2):
             d1 = flavours[f][0]
-            start, landed, _ = piece(p, f)
-            landed(1)
+            start = piece(p, f)
             total = part[w, f, d1].astype(F32) + r2[w, f, 0].astype(F32) + r2[w, f, 1].astype(F32)
             summed[w, f] = total.astype(BF)
             start(6, 7, 8, 9)
 
     def stage_d(p):
         w = lax.rem(p, RING)
+        landed(p, 2)
+        sent(p, 0)
         for f in range(2):
             d2 = flavours[f][1]
-            start, landed, _ = piece(p, f)
-            landed(2)
+            start = piece(p, f)
             n2, b2 = plus(d2), minus(d2)
             summed[w, f, n2, 0:32] = (summed[w, f, n2, 0:32].astype(F32) + t1[w, f, 0].astype(F32)).astype(BF)
             summed[w, f, b2, 32:64] = (summed[w, f, b2, 32:64].astype(F32) + t1[w, f, 1].astype(F32)).astype(BF)
@@ -354,43 +387,40 @@
 
     def stage_e(p):
         w, v = lax.rem(p, RING), lax.rem(p, HELD)
+        landed(p, 3)
         j = lax.rem(p, NJ)
         on_pre = (p >= NJ).astype(F32)
         for f in range(2):
             d1, d2 = flavours[f][:2]
-            start, landed, sent = piece(p, f)
-            landed(3)
+            start = piece(p, f)
             total = summed[w, f, d2].astype(F32) + t2[w, f, 0].astype(F32) + t2[w, f, 1].astype(F32)
             lanes = pl.ds(pl.multiple_of(j * WIDE + f * HALF, HALF), HALF)
             total = total + bias[0:1, lanes] * on_pre
             full[v, f, d1, d2] = (keep[:, lanes] * total).astype(BF)
             start(12, 13)
-            sent(0)
 
     def stage_f(p):
-        for f in range(2):
-            start, landed, _ = piece(p, f)
-            landed(4)
+        landed(p, 4)
+        sent(p, 1)
+        for f in range(2):
+            start = piece(p, f)
             start(14, 15)
 
     def stage_g(p):
-        for f in range(2):
-            start, landed, sent = piece(p, f)
-            landed(5)
+        landed(p, 5)
+        for f in range(2):
+            start = piece(p, f)
             start(16, 17)
-            sent(1)
 
     def stage_h(p):
-        for f in range(2):
-            start, landed, _ = piece(p, f)
-            landed(6)
+        landed(p, 6)
+        for f in range(2):
+            start = piece(p, f)
             start(18, 19)
 
     def stage_m(p):
         w = lax.rem(p, HELD)
-        for f in range(2):
-            _, landed, _ = piece(p, f)
-            landed(7)
+        landed(p, 7)
         for f in range(2):
             for q in range(4):
                 for k in range(4):
@@ -415,9 +445,7 @@
             res = lax.dot_general(cols[...], grd[...], (((0,), (0,)), ((), ())), preferred_element_type=F32)
             gd_out[pl.ds(pl.multiple_of(j * WIDE, WIDE), WIDE), :] = (res * SCALE).astype(BF)
 
-        for f in range(2):
-            _, _, sent = piece(p, f)
-            sent(2)
+        sent(p, 2)
 
     def gt_copies():
         s, r = gt_s, gt_r
@@ -436,7 +464,7 @@
 
         def send(k):
             a, b, dev = sends[k]
-            return remote(a, b, s.at[k], r.at[k], dev)
+            return remote(a, b, s, r.at[k], dev)
 
         return send
 
@@ -468,14 +496,10 @@
         for k in (3, 4, 5, 6):
             send(k).wait_recv()
         gt_out[...] = (gtp[c, z].astype(F32) + z2[0].astype(F32) + z2[1].astype(F32)).astype(BF)
-        for k in range(7):
-            send(k).wait_send()
+        size = tok.at[pl.ds(0, 896)]
+        remote(size, size, gt_s, gt_r.at[0], sib).wait_send()
 
     def step(i, carry):
-        @pl.when(i >= SLACK)
-        def _():
-            pl.semaphore_wait(pace, 1)
-
         for fn, lag in (
             (stage_h, LAG_H), (stage_g, LAG_G), (stage_f, LAG_F), (stage_e, LAG_E),
             (stage_d, LAG_D), (stage_c, LAG_C), (stage_b, LAG_B), (stage_a, LAG_A), (stage_m, LAG_M),
@@ -518,11 +542,9 @@
         at(last + 2)(gt_1)
         at(last + 4)(gt_2)
         at(last + 7)(gt_3)
-        pl.semaphore_signal(pace, inc=1, device_id=sib, device_id_type=MESH)
         return carry
 
     lax.fori_loop(0, NP + LAG_M, step, 0)
-    pl.semaphore_wait(pace, SLACK)
 
 
 def flush(gt, gu, gd, gb, gt_out, gu_out, gd_out, gb_out, sem):
@@ -572,15 +594,14 @@
             pltpu.VMEM((64, FB // 16), jnp.int32),
             pltpu.VMEM((64, FB // 16), jnp.int32),
             pltpu.VMEM((1, FB), F32),
-            dma((HELD, 2, 3)),
-            dma((HELD, 2, 8)),
+            dma((N_SEND,)),
+            dma((N_RECV,)),
+            dma((2,)),
             dma((2, 11)),
-            dma((2, 11)),
-            dma((7,)),
+            dma,
             dma((7,)),
             dma,
             dma,
-            pltpu.SemaphoreType.REGULAR,
             dma((8,)),
         ],
         compiler_params=pltpu.CompilerParams(

time: 155 us -> 151 us (0.974); the launches traced: 153 us -> 151 us
  Pallas kernels: 153 us -> 151 us
    pallas_call x1, Pallas kernels: 149 us -> 147 us  [body(): pl.pallas_call(kernel, out_shape=tuple((pltpu.VMEM(shape, dtype) for shap...]
where the time goes in v3:
time: 151 us
  Pallas kernels  151 us (100%)
    pallas_call x1, Pallas kernels, body(): pl.pallas_call(kernel, out_shape=tuple((pltpu.VMEM(shape, dtype) for shap...  147 us
    pallas_call x1, Pallas kernels, body(): pl.pallas_call(flush, out_shape=tuple((jax.ShapeDtypeStruct(shape, dtype)...  3.79 us

profile of v3, /device:TPU:0, one launch (start us, length us, event | category | flops | bytes accessed | tf_op | source)
XLA Modules:
  0.0 151.3 jit_solution(11829562954530620685)
XLA Ops:
  0.6 146.9 %fused.1 = (bf16[128,768]{1,0:T(8,128)(2,1)S(1)}, bf16[768,3072]{1,0:T(8,128)(2,1)S(1)}, bf16[3072,768]{1,0:T(8,128)(2,1)S(1)}, f32[1,3072]{1,0:T(1,128)S(1)}) custom-call(bf16[128,768]{1,0:T(8,128)(2,1)} %tok_hbm.1, bf16[128,768]{1,0:T(8,128)(2,1)} %grd_hbm.1, bf16[768,3072]{1,0:T(8,128)(2,1)} %up_hbm.1, bf16[3072,768]{1,0:T(8,128)(2,1)} %down_hbm.1, ...), custom_call_target="tpu_custom_call" | custom-call | flops 24159191040 | bytes 23592960 | tf_op jit(solution)/shard_map/fused/pallas_call | solution.py:568
  147.5 3.8 %flush.1 = (bf16[128,768]{1,0:T(8,128)(2,1)}, bf16[768,3072]{1,0:T(8,128)(2,1)}, bf16[3072,768]{1,0:T(8,128)(2,1)}, f32[1,3072]{1,0:T(1,128)}) custom-call(bf16[128,768]{1,0:T(8,128)(2,1)S(1)} %get-tuple-element.12.gt, bf16[768,3072]{1,0:T(8,128)(2,1)S(1)} %get-tuple-element.13.gu, bf16[3072,768]{1,0:T(8,128)(2,1)S(1)} %get-tuple-element.14.gd, ...), custom_call_target="tpu_custom_call" | custom-call | tf_op jit(solution)/shard_map/flush/pallas_call | solution.py:615

commit v4 on v3

--- a/solution.py
+++ b/solution.py
@@ -19,14 +19,15 @@
 RING = 16
 HELD = 16
 EARLY = 8
+LATE = 2
 KEEP = 1.0 / 0.9
 SCALE = 1.0 / math.sqrt(TOK)
 BF = jnp.bfloat16
 F32 = jnp.float32
-GROUP = (0, 0, 1, 1, 1, 1, 2, 2, 3, 3, 3, 3, 4, 4, 5, 5, 6, 6, 7, 7)
-RECV_RING = ((0, 12), (12, 12), (24, 6), (30, 6), (36, 6), (42, 6), (48, 6), (54, 6))
+GROUP = (0, 0, 1, 1, 1, 1, 2, 2, 3, 3, 3, 3, 4, 4, 5, 5, 6, 6, 7, 7, 7)
+RECV_RING = ((0, 12), (12, 12), (24, 6), (30, 6), (36, 6), (42, 6), (48, 6), (54, 12))
 SEND_RING = ((0, 12), (12, 6), (18, 12))
-N_RECV, N_SEND = 60, 30
+N_RECV, N_SEND = 66, 30
 LAG_A, LAG_B, LAG_C, LAG_D, LAG_E, LAG_F, LAG_G, LAG_H, LAG_M = -EARLY, 0, 2, 4, 6, 8, 10, 12, 14
 
 
@@ -36,8 +37,8 @@
 
 def kernel(
     tok_hbm, grd_hbm, up_hbm, down_hbm, bias_hbm, relu_hbm, drop_hbm,
-    gt_out, gu_out, gd_out, gb_out,
-    tok, grd, tok_t, up, down, keep, acc, cols,
+    gt_out, gu_out, gd_out, gb_out, late, grd,
+    tok, tok_t, up, down, keep, acc, cols,
     part, r1, r2, summed, t1, t2, full,
     gtp, gtr, z1, z2, words, dropped, swapped, bias,
     ss, rs, ag_s, ag_r, gt_s, gt_r, sw_s, sw_r, loc,
@@ -59,7 +60,8 @@
     yp, ym = (x * 4 + plus(y), col), (x * 4 + minus(y), col)
     zp, zm = (row, plus(z) * 2 + c), (row, minus(z) * 2 + c)
     sib = (row, z * 2 + (1 - c))
-    everyone = (xp, xm, yp, ym, zp, zm, sib)
+    xf, yf = (far(x) * 4 + y, col), (x * 4 + far(y), col)
+    everyone = (xp, xm, yp, ym, zp, zm, sib, xf, yf)
 
     def remote(src, dst, s, r, dev):
         return pltpu.make_async_remote_copy(
@@ -192,7 +194,7 @@
             on = (picked >> (bit % 8)) & 1
             keep[:, pl.ds(pl.multiple_of(j * WIDE + f * HALF, HALF), HALF)] = on.astype(F32) * KEEP
 
-    flavours = ((x, y, xp, xm, yp, ym), (y, x, yp, ym, xp, xm))
+    flavours = ((x, y, xp, xm, yp, ym, xf), (y, x, yp, ym, xp, xm, yf))
 
     def send_sem(p, n):
         first, length = SEND_RING[n]
@@ -271,7 +273,7 @@
 
         u = (t * 4) // 5
         first = (t == 1).astype(jnp.int32) * (EARLY // 2)
-        end = EARLY - (t == 0).astype(jnp.int32) * (EARLY - EARLY // 2)
+        end = EARLY + (t == 1).astype(jnp.int32) * (NJ - EARLY) - (t == 0).astype(jnp.int32) * (EARLY - EARLY // 2)
         early(lax.rem(z + u + u // 2 - 2 * (u // 3), 4), first, end)
         return carry
 
@@ -280,7 +282,7 @@
     loads[7].wait()
 
     def piece(p, f):
-        d1, d2, p1, m1, p2, m2 = flavours[f]
+        d1, d2, p1, m1, p2, m2, f1 = flavours[f]
         w, v = lax.rem(p, RING), lax.rem(p, HELD)
         pt, sm, g = part.at[w, f], summed.at[w, f], full.at[v, f]
         ra, rb, ta, tb = r1.at[w, f], r2.at[w, f], t1.at[w, f], t2.at[w, f]
@@ -309,6 +311,7 @@
             (g.at[d1], g.at[d1], m1),
             (g.at[b1, lo], g.at[b1, lo], p1),
             (g.at[n1, hi], g.at[n1, hi], m1),
+            (g.at[d1], g.at[d1], f1),
         )
 
         def start(*ks):
@@ -332,25 +335,23 @@
         p = i - lag
         return p, (p >= 0) & (p < NP)
 
-    def forward(p, left, weight):
-        for q in range(4):
-            forward_block(p, left, weight, q)
-
     def stage_a(p):
-
         @pl.when(p < NJ)
         def _():
-            rows = down[pl.ds(pl.multiple_of(p * WIDE, WIDE), WIDE), :]
-            forward(p, grd, lambda left: dot_nt(left, rows))
+            def other(n, carry):
+                early(lax.rem(z + n, 4), p, p + 1)
+                return carry
+
+            lax.fori_loop(1, 4, other, 0)
 
         @pl.when(p >= NJ)
         def _():
             lanes = up[:, pl.ds(pl.multiple_of((p - NJ) * WIDE, WIDE), WIDE)]
-            forward(p, tok, lambda left: jnp.dot(left, lanes, preferred_element_type=F32))
-
-        for f in range(2):
-            start = piece(p, f)
-            start(0, 1, 2, 3)
+            for q in range(4):
+                forward_block(p, tok, lambda left: jnp.dot(left, lanes, preferred_element_type=F32), q)
+            for f in range(2):
+                start = piece(p, f)
+                start(0, 1, 2, 3)
 
     def stage_b(p):
         w = lax.rem(p, RING)
@@ -411,20 +412,24 @@
         for f in range(2):
             start = piece(p, f)
             start(16, 17)
+            pl.when(p >= NP - LATE)(functools.partial(start, 20))
 
     def stage_h(p):
         landed(p, 6)
         for f in range(2):
             start = piece(p, f)
-            start(18, 19)
-
-    def stage_m(p):
+            pl.when(p < NP - LATE)(functools.partial(start, 18, 19))
+
+    def collect(p, ref):
         w = lax.rem(p, HELD)
         landed(p, 7)
         for f in range(2):
             for q in range(4):
                 for k in range(4):
-                    cols[(q * 4 + k) * 64 : (q * 4 + k + 1) * 64, f * HALF : (f + 1) * HALF] = full[w, f, k, q]
+                    ref[(q * 4 + k) * 64 : (q * 4 + k + 1) * 64, f * HALF : (f + 1) * HALF] = full[w, f, k, q]
+
+    def stage_m(p):
+        collect(p, cols)
 
         @pl.when(p < NJ)
         def _():
@@ -515,12 +520,11 @@
         def _():
             swap.wait()
 
-        pl.when(i < NJ)(functools.partial(unpack, i))
+        pl.when((i >= 5) & (i < NJ + 5))(functools.partial(unpack, i - 5))
 
         @at(0)
         def _():
             gather_1(1, tok_hbm, tok)
-            acc[...] = jnp.zeros_like(acc)
 
         @at(2)
         def _():
@@ -532,8 +536,9 @@
         def _():
             gather_3(1, tok_hbm, tok)
 
-        @at(6)
-        def _():
+        @at(12)
+        def _():
+            acc[...] = jnp.zeros_like(acc)
             for q in range(8):
                 tok_t[:, q * 128 : (q + 1) * 128] = tok[q * 128 : (q + 1) * 128, :].T
 
@@ -544,18 +549,28 @@
         at(last + 7)(gt_3)
         return carry
 
-    lax.fori_loop(0, NP + LAG_M, step, 0)
-
-
-def flush(gt, gu, gd, gb, gt_out, gu_out, gd_out, gb_out, sem):
+    lax.fori_loop(0, NP + LAG_H, step, 0)
+    for k in range(LATE):
+        collect(NP - LATE + k, late.at[k])
+        sent(NP - LATE + k, 2)
+
+
+def flush(gt, gu, gd, gb, late, grd, gt_out, gu_out, gd_out, gb_out, rows, sem):
+    done = FB - LATE * WIDE
     copies = [pltpu.make_async_copy(gt, gt_out, sem.at[0]), pltpu.make_async_copy(gb, gb_out, sem.at[1])]
     for q in range(4):
-        rows = pl.ds(q * DB // 4, DB // 4)
-        copies.append(pltpu.make_async_copy(gu.at[rows], gu_out.at[rows], sem.at[2 + q]))
-        rows = pl.ds(q * FB // 4, FB // 4)
-        copies.append(pltpu.make_async_copy(gd.at[rows], gd_out.at[rows], sem.at[6 + q]))
+        part = pl.ds(q * DB // 4, DB // 4)
+        copies.append(pltpu.make_async_copy(gu.at[part], gu_out.at[part], sem.at[2 + q]))
+        part = pl.ds(q * done // 4, done // 4)
+        copies.append(pltpu.make_async_copy(gd.at[part], gd_out.at[part], sem.at[6 + q]))
     for cp in copies:
         cp.start()
+    for k in range(LATE):
+        res = lax.dot_general(late[k], grd[...], (((0,), (0,)), ((), ())), preferred_element_type=F32)
+        rows[k] = (res * SCALE).astype(BF)
+        cp = pltpu.make_async_copy(rows.at[k], gd_out.at[pl.ds(done + k * WIDE, WIDE)], sem.at[10 + k])
+        cp.start()
+        copies.append(cp)
     for cp in copies:
         cp.wait()
 
@@ -565,13 +580,13 @@
     vmem = pl.BlockSpec(memory_space=pltpu.VMEM)
     dma = pltpu.SemaphoreType.DMA
     shapes = (((128, DB), BF), ((DB, FB), BF), ((FB, DB), BF), ((1, FB), F32))
+    kept = (((LATE, TOK, WIDE), BF), ((TOK, DB), BF))
     held = pl.pallas_call(
         kernel,
-        out_shape=tuple(pltpu.VMEM(shape, dtype) for shape, dtype in shapes),
+        out_shape=tuple(pltpu.VMEM(shape, dtype) for shape, dtype in shapes + kept),
         in_specs=[hbm] * 7,
-        out_specs=(vmem,) * 4,
+        out_specs=(vmem,) * 6,
         scratch_shapes=[
-            pltpu.VMEM((TOK, DB), BF),
             pltpu.VMEM((TOK, DB), BF),
             pltpu.VMEM((DB, TOK), BF),
             pltpu.VMEM((DB, FB), BF),
@@ -615,10 +630,10 @@
     gt, gu, gd, gb = pl.pallas_call(
         flush,
         out_shape=tuple(jax.ShapeDtypeStruct(shape, dtype) for shape, dtype in shapes),
-        in_specs=[vmem] * 4,
+        in_specs=[vmem] * 6,
         out_specs=(hbm,) * 4,
-        scratch_shapes=[dma((10,))],
-        compiler_params=pltpu.CompilerParams(vmem_limit_bytes=2**20),
+        scratch_shapes=[pltpu.VMEM((LATE, WIDE, DB), BF), dma((10 + LATE,))],
+        compiler_params=pltpu.CompilerParams(vmem_limit_bytes=6 * 2**20),
         name="flush",
     )(*held)
     return gt, gu, gd, gb.reshape(FB)

time: 151 us -> 150 us (level)
  Pallas kernels: 151 us -> 149 us
    pallas_call x1, Pallas kernels: 147 us -> 145 us  [body(): pl.pallas_call(kernel, out_shape=tuple((pltpu.VMEM(shape, dtype) for shap...]
where the time goes in v4:
time: 150 us; the launch traced here: 149 us
  Pallas kernels  149 us (99%)
    pallas_call x1, Pallas kernels, body(): pl.pallas_call(kernel, out_shape=tuple((pltpu.VMEM(shape, dtype) for shap...  145 us
    pallas_call x1, Pallas kernels, body(): pl.pallas_call(flush, out_shape=tuple((jax.ShapeDtypeStruct(shape, dtype)...  3.78 us

profile of v4, /device:TPU:0, one launch (start us, length us, event | category | flops | bytes accessed | tf_op | source)
XLA Modules:
  0.0 149.2 jit_solution(16830093231366967525)
XLA Ops:
  0.6 144.7 %fused.1 = (bf16[128,768]{1,0:T(8,128)(2,1)S(1)}, bf16[768,3072]{1,0:T(8,128)(2,1)S(1)}, bf16[3072,768]{1,0:T(8,128)(2,1)S(1)}, f32[1,3072]{1,0:T(1,128)S(1)}, b...) custom-call(bf16[128,768]{1,0:T(8,128)(2,1)} %tok_hbm.1, bf16[128,768]{1,0:T(8,128)(2,1)} %grd_hbm.1, ...), custom_call_target="tpu_custom_call" | custom-call | flops 24159191040 | bytes 23592960 | tf_op jit(solution)/shard_map/fused/pallas_call | solution.py:584
  145.4 3.8 %flush.1 = (bf16[128,768]{1,0:T(8,128)(2,1)}, bf16[768,3072]{1,0:T(8,128)(2,1)}, bf16[3072,768]{1,0:T(8,128)(2,1)}, f32[1,3072]{1,0:T(1,128)}) custom-call(bf16[128,768]{1,0:T(8,128)(2,1)S(1)} %get-tuple-element.14.gt, bf16[768,3072]{1,0:T(8,128)(2,1)S(1)} %get-tuple-element.15.gu, bf16[3072,768]{1,0:T(8,128)(2,1)S(1)} %get-tuple-element.16.gd, ...), custom_call_target="tpu_custom_call" | custom-call | tf_op jit(solution)/shard_map/flush/pallas_call | solution.py:630

commit v5 on v4

--- a/solution.py
+++ b/solution.py
@@ -211,12 +211,19 @@
             for k in range(4):
                 part[w, f, k, q] = res[k * 64 : (k + 1) * 64, f * HALF : (f + 1) * HALF]
 
-    def early(q, first, end):
+    def early(q, first, end, pieces=1):
         top = q // 2
 
-        def one(p, carry):
-            rows = down[pl.ds(pl.multiple_of(p * WIDE, WIDE), WIDE), :]
-            forward_block(p, grd, lambda left: dot_nt(left, rows), q)
+        def several(n, carry):
+            for k in range(pieces):
+                p = n * pieces + k
+                rows = down[pl.ds(pl.multiple_of(p * WIDE, WIDE), WIDE), :]
+                forward_block(p, grd, functools.partial(dot_nt, right=rows), q)
+            for k in range(pieces):
+                send_block(n * pieces + k)
+            return carry
+
+        def send_block(p):
             for f in range(2):
                 d1 = flavours[f][0]
                 pt, ra, rb = part.at[p, f], r1.at[p, f], r2.at[p, f]
@@ -229,9 +236,8 @@
                 remote(pt.at[far(d1), q], ra.at[top, q - 2 * top], send_sem(p, 0), recv_sem(p, 0), dev).start()
                 to, dev = along(3 - 2 * top)
                 remote(pt.at[to, q], rb.at[1 - top, q], send_sem(p, 0), recv_sem(p, 1), dev).start()
-            return carry
-
-        lax.fori_loop(first, end, one, 0)
+
+        lax.fori_loop(first // pieces, end // pieces, several, 0)
 
     loads[0].wait()
     loads[1].wait()
@@ -274,7 +280,7 @@
         u = (t * 4) // 5
         first = (t == 1).astype(jnp.int32) * (EARLY // 2)
         end = EARLY + (t == 1).astype(jnp.int32) * (NJ - EARLY) - (t == 0).astype(jnp.int32) * (EARLY - EARLY // 2)
-        early(lax.rem(z + u + u // 2 - 2 * (u // 3), 4), first, end)
+        early(lax.rem(z + u + u // 2 - 2 * (u // 3), 4), first, end, 2)
         return carry
 
     lax.fori_loop(0, 5, arrive, 0)

time: 150 us -> 149 us (level)
  no operation moved by 1% of the time
where the time goes in v5:
time: 149 us
  Pallas kernels  148 us (99%)
    pallas_call x1, Pallas kernels, body(): pl.pallas_call(kernel, out_shape=tuple((pltpu.VMEM(shape, dtype) for shap...  144 us
    pallas_call x1, Pallas kernels, body(): pl.pallas_call(flush, out_shape=tuple((jax.ShapeDtypeStruct(shape, dtype)...  3.78 us

profile of v5, /device:TPU:0, one launch (start us, length us, event | category | flops | bytes accessed | tf_op | source)
XLA Modules:
  0.0 148.5 jit_solution(17915938737947857858)
XLA Ops:
  0.6 144.1 %fused.1 = (bf16[128,768]{1,0:T(8,128)(2,1)S(1)}, bf16[768,3072]{1,0:T(8,128)(2,1)S(1)}, bf16[3072,768]{1,0:T(8,128)(2,1)S(1)}, f32[1,3072]{1,0:T(1,128)S(1)}, b...) custom-call(bf16[128,768]{1,0:T(8,128)(2,1)} %tok_hbm.1, bf16[128,768]{1,0:T(8,128)(2,1)} %grd_hbm.1, ...), custom_call_target="tpu_custom_call" | custom-call | flops 24159191040 | bytes 23592960 | tf_op jit(solution)/shard_map/fused/pallas_call | solution.py:590
  144.7 3.8 %flush.1 = (bf16[128,768]{1,0:T(8,128)(2,1)}, bf16[768,3072]{1,0:T(8,128)(2,1)}, bf16[3072,768]{1,0:T(8,128)(2,1)}, f32[1,3072]{1,0:T(1,128)}) custom-call(bf16[128,768]{1,0:T(8,128)(2,1)S(1)} %get-tuple-element.14.gt, bf16[768,3072]{1,0:T(8,128)(2,1)S(1)} %get-tuple-element.15.gu, bf16[3072,768]{1,0:T(8,128)(2,1)S(1)} %get-tuple-element.16.gd, ...), custom_call_target="tpu_custom_call" | custom-call | tf_op jit(solution)/shard_map/flush/pallas_call | solution.py:636
